TPU v7x, 512 devices: a whole 4x4x16 slice. The times are simulated.
512 devices in a mesh: ctx: 8 (over y, core), exp: 64 (over z, x).
Axes of the slice: x: 4, y: 4, z: 16, core: 2. Of those that a mesh axis runs over, the one named last changes fastest.
Arguments:
- prefill_cache: bfloat16 [512, 512, 576], P('ctx', 'exp'), may hold values from -600 to 600
- owner_slot: int32 [512], replicated, may hold values from 0 to 511, as said below
- cached_len: int32 [512], replicated, may hold values from 1 to 512
- query_latent: bfloat16 [512, 1536], P('ctx'), may hold values from -6 to 6
- new_latent: bfloat16 [512, 576], P('ctx'), may hold values from -6 to 6
- wq_up: bfloat16 [1536, 64, 192], P(None, 'exp'), may hold values from -0.15625 to 0.15625
- wk_up: bfloat16 [64, 128, 512], P('exp'), may hold values from -0.5 to 0.5
- wv_up: bfloat16 [64, 512, 128], P('exp'), may hold values from -0.25 to 0.25
- w_out: bfloat16 [8192, 7168], P('exp'), may hold values from -0.0625 to 0.0625
- residual: bfloat16 [512, 7168], P(('ctx', 'exp')), may hold values from -6 to 6
- ffn_gain: float32 [7168], replicated, may hold values from 0.5 to 1.5
- expert_ids: int32 [512, 8], P('ctx'), may hold values from 0 to 255, all different within a row; in each aligned block of 64 rows (0 to 63, 64 to 127, ...) at most 4 rows name the same one
Outputs:
- hidden_out: bfloat16 [512, 7168], P(('ctx', 'exp'))
- expert_in: bfloat16 [8, 256, 4, 7168], P('ctx', 'exp')
Inputs may be any that keep to these rules, and one draw needn't show every extreme that they name: A permutation of decode rows; request r goes to owner owner_slot[r] // 64. The 64 requests of one prefill shard (r // 64 equal) send at most 16 to one owner, and some shard sends exactly 16 to some owner. `expert_ids`: in each aligned block of 64 rows (one owner) no expert is chosen by more than 4 rows.
All inputs are finite; a program needn't handle non-finite values.
Results may differ from a plain program's by a relative error of at most 0.008.
Values may be sent and summed in bfloat16 or wider, within the bound.
A program may use at most 64 MiB of HBM per device.

v0:
```python
import math

import jax
import jax.numpy as jnp
from jax import lax
from jax.sharding import PartitionSpec as P

EXPERTS = 256
CAP = 4


def rotate(part, positions):
    half = part.shape[-1] // 2
    index = jnp.arange(half, dtype=jnp.float32)
    freqs = 10000.0 ** (-2.0 * index / part.shape[-1])
    angles = positions.astype(jnp.float32)[:, None, None] * freqs
    first = part[..., :half]
    second = part[..., half:]
    return jnp.concatenate(
        [
            first * jnp.cos(angles) - second * jnp.sin(angles),
            first * jnp.sin(angles) + second * jnp.cos(angles),
        ],
        -1,
    )


def normalize(hidden, ffn_gain):
    return (
        hidden * lax.rsqrt(jnp.mean(hidden * hidden, -1, keepdims=True) + 1e-06) * ffn_gain
    ).astype(jnp.bfloat16)


def on_device(
    prefill_cache,
    owner_slot,
    cached_len,
    query_latent,
    new_latent,
    wq_up,
    wk_up,
    wv_up,
    w_out,
    residual,
    ffn_gain,
    expert_ids,
):
    shards = lax.axis_size("exp")
    group = lax.axis_index("ctx")
    shard = lax.axis_index("exp")
    rows = query_latent.shape[0]
    tokens = prefill_cache.shape[1]
    latent_width = prefill_cache.shape[2]
    total = owner_slot.shape[0]
    nope = wk_up.shape[1]
    kvl = wk_up.shape[2]
    heads_dev = wv_up.shape[0]
    value_width = wv_up.shape[2]
    request = jnp.arange(total, dtype=jnp.int32)
    slots = group * rows + jnp.arange(rows, dtype=jnp.int32)
    match = owner_slot[None, :] == slots[:, None]
    anchor = jnp.sum(jnp.where(match, request[None, :], 0), 1)
    lengths = jnp.sum(jnp.where(match, cached_len[None, :], 0), 1)
    flat_cache = prefill_cache.reshape(rows, tokens * latent_width)
    whole = lax.all_gather(flat_cache, "ctx", axis=0, tiled=True)
    pick = (anchor[:, None] == request[None, :]).astype(jnp.bfloat16)
    cache = jnp.dot(pick, whole, preferred_element_type=jnp.float32)
    cache = cache.astype(jnp.bfloat16).reshape(rows, tokens, latent_width)
    q_local = jnp.einsum(
        "rq,qhd->rhd", query_latent, wq_up, preferred_element_type=jnp.float32
    ).astype(jnp.bfloat16)
    q_abs = jnp.einsum(
        "rhn,hnc->rhc", q_local[..., :nope], wk_up, preferred_element_type=jnp.float32
    )
    absorbed = jnp.concatenate(
        [q_abs, rotate(q_local[..., nope:].astype(jnp.float32), lengths)], -1
    ).astype(jnp.bfloat16)
    scale = 1.0 / math.sqrt(q_local.shape[2])
    queries = lax.all_gather(absorbed, "exp", axis=1, tiled=True)
    scores = jnp.einsum("rhc,rlc->rhl", queries, cache, preferred_element_type=jnp.float32) * scale
    new_scores = (
        jnp.einsum("rhc,rc->rh", queries, new_latent, preferred_element_type=jnp.float32) * scale
    )
    position = shard * tokens + jnp.arange(tokens, dtype=jnp.int32)
    valid = (position[None, :] < lengths[:, None])[:, None, :]
    first = shard == 0
    local_max = jnp.max(jnp.where(valid, scores, -1e30), 2)
    top = jnp.where(first, jnp.maximum(local_max, new_scores), local_max)
    weights = jnp.where(valid, jnp.exp(scores - top[..., None]), 0.0)
    new_weight = jnp.where(first, jnp.exp(new_scores - top), 0.0)
    total_weight = jnp.sum(weights, 2) + new_weight
    mixed = jnp.einsum(
        "rhl,rlc->rhc",
        weights.astype(jnp.bfloat16),
        cache[..., :kvl],
        preferred_element_type=jnp.float32,
    )
    new_rounded = lax.optimization_barrier(new_weight.astype(jnp.bfloat16))
    mixed = (
        mixed
        + new_rounded.astype(jnp.float32)[..., None] * new_latent[:, None, :kvl].astype(jnp.float32)
    ).astype(jnp.bfloat16)
    parts = lax.all_to_all(mixed, "exp", split_axis=1, concat_axis=0, tiled=True).reshape(
        shards, rows, heads_dev, kvl
    )
    maxima, totals = (
        lax.all_to_all(top, "exp", split_axis=1, concat_axis=0, tiled=True),
        lax.all_to_all(total_weight, "exp", split_axis=1, concat_axis=0, tiled=True),
    )
    maxima = maxima.reshape(shards, rows, heads_dev)
    totals = totals.reshape(shards, rows, heads_dev)
    peak = jnp.max(maxima, 0)
    factors = jnp.exp(maxima - peak)
    numer = jnp.einsum("srh,srhc->rhc", factors, parts.astype(jnp.float32))
    denom = jnp.sum(factors * totals, 0)
    latent_out = (numer / denom[..., None]).astype(jnp.bfloat16)
    heads_out = (
        jnp.einsum("rhc,hcv->rhv", latent_out, wv_up, preferred_element_type=jnp.float32)
        .astype(jnp.bfloat16)
        .reshape(rows, heads_dev * value_width)
    )
    attn_rows = lax.psum_scatter(
        jnp.dot(heads_out, w_out, preferred_element_type=jnp.float32),
        "exp",
        scatter_dimension=0,
        tiled=True,
    )
    hidden = residual.astype(jnp.float32) + attn_rows
    normed = lax.all_gather(normalize(hidden, ffn_gain), "exp", axis=0, tiled=True)
    hidden_rows = hidden.astype(jnp.bfloat16)
    experts_dev = EXPERTS // shards
    names = jnp.sum(
        (expert_ids[:, :, None] == jnp.arange(EXPERTS, dtype=jnp.int32)[None, None, :]).astype(
            jnp.int32
        ),
        1,
    )
    before = jnp.cumsum(names, 0) - names
    mine = lax.dynamic_slice_in_dim(names, shard * experts_dev, experts_dev, 1)
    mine_slot = lax.dynamic_slice_in_dim(before, shard * experts_dev, experts_dev, 1)
    slot_ids = jnp.arange(CAP, dtype=jnp.int32)
    pick = (
        (mine.T[:, None, :] == 1) & (mine_slot.T[:, None, :] == slot_ids[None, :, None])
    ).astype(jnp.bfloat16)
    expert_in = jnp.einsum("xso,od->xsd", pick, normed, preferred_element_type=jnp.float32).astype(
        jnp.bfloat16
    )
    return (hidden_rows, expert_in[None])


def solution(mesh):
    placed = (
        P("ctx", "exp", None),
        P(),
        P(),
        P("ctx", None),
        P("ctx", None),
        P(None, "exp", None),
        P("exp", None, None),
        P("exp", None, None),
        P("exp", None),
        P(("ctx", "exp"), None),
        P(),
        P("ctx", None),
    )
    return jax.shard_map(
        on_device,
        mesh=mesh,
        in_specs=placed,
        out_specs=(P(("ctx", "exp"), None), P("ctx", "exp", None, None)),
        check_vma=False,
    )
```

profile of v0, /device:TPU:16, one launch (start us, length us, event | category | flops | bytes accessed | tf_op | source)
XLA Modules:
  0.0 839.2 jit_solution(8072667432537616847)
XLA Ops:
  7.2 2.4 reshape.259
  9.7 0.9 fusion.20
  10.6 1.5 fusion.11
  12.1 0.1 fusion.42
  12.5 1.1 fusion.10
  13.6 0.7 pad_maximum_fusion
  14.4 40.8 %all-gather.6.cloned.1.call-done = bf16[512,4608]{1,0:T(8,128)(2,1)} async-done(((bf16[64,4608]{1,0:T(8,128)(2,1)}), bf16[512,4608]{1,0:T(8,128)(2,1)}) %all-gather.6.cloned.1.call-update) | async-done | bytes 4718608 | tf_op jit(solution)/shard_map/all_gather | solution.py:65
  55.2 3.3 convolution_convert_fusion.1
  58.5 0.5 reshape.260
  59.0 151.0 %all-gather.4.cloned.1.call-done = bf16[64,64,576]{2,0,1:T(8,128)(2,1)} async-done(((bf16[64,1,576]{2,0,1:T(8,128)(2,1)}), bf16[64,64,576]{2,0,1:T(8,128)(2,1)}) %all-gather.4.cloned.1.call-update) | async-done | bytes 4718608 | tf_op jit(solution)/shard_map/all_gather | solution.py:79
  210.0 5.8 fusion.1
  215.8 3.2 select_reduce_fusion
  219.1 0.2 fusion.17
  219.3 0.7 copy.54
  220.0 8.3 all-to-all-start.2
  228.3 0.7 copy.52
  229.0 13.8 %all-to-all-done.2 = f32[64,64,1]{0,2,1:T(1,128)S(1)} async-done(((f32[64,64,1]{0,2,1:T(1,128)}), f32[64,64,1]{0,2,1:T(1,128)S(1)}, u32[]{:S(2)}, u32[]{:S(2)}) %all-to-all-start.2) | async-done | bytes 16416 | tf_op jit(solution)/shard_map/all_to_all | solution.py:108
  242.8 4.7 all-to-all-start
  247.5 2.3 add_convert_fusion
  249.8 4.3 copy.53
  254.1 7.8 all-to-all-done
  261.9 7.4 all-to-all-start.1
  269.7 176.1 %all-to-all-done.1 = bf16[64,64,512]{2,0,1:T(8,128)(2,1)} async-done(((bf16[64,64,512]{2,0,1:T(8,128)(2,1)}), bf16[64,64,512]{2,0,1:T(8,128)(2,1)}, u32[]{:S(2)}, u32[]{:S(2)}) %all-to-all-start.1) | async-done | bytes 4194336 | tf_op jit(solution)/shard_map/all_to_all | solution.py:103
  445.8 6.7 fusion.5
  452.5 1.8 fusion.12
  454.4 0.2 convert_reduce_fusion
  455.1 1.3 dynamic-slice
  456.4 271.5 %all-reduce.3.cloned.1.call-done = f32[64,7168]{1,0:T(8,128)} async-done(((f32[64,7168]{1,0:T(8,128)}), f32[64,7168]{1,0:T(8,128)}) %all-reduce.3.cloned.1.call-update) | async-done | bytes 1835024
  727.9 2.3 multiply_reduce_fusion
  730.9 0.7 convert_bitcast_fusion
  731.5 100.1 %all-gather = bf16[64,1,7168]{2,1,0:T(2,128)(2,1)S(1)} all-gather(bf16[1,1,7168]{2,1,0:T(2,128)(2,1)S(1)} %get-tuple-element.12), channel_id=1, replica_groups=mesh['ctx'=8,'exp'=64] {'exp'}, dimensions={0}, use_global_device_ids=true | all-gather | bytes 931840 | tf_op jit(solution)/shard_map/all_gather | solution.py:129
  831.6 1.1 fusion
  (41 shorter events, 1.3 us)
Async XLA Ops:
  7.2 445.3 %copy-start = (bf16[128,7168]{1,0:T(8,128)(2,1)S(1)}, bf16[128,7168]{1,0:T(8,128)(2,1)}, u32[]{:S(2)}) copy-start(bf16[128,7168]{1,0:T(8,128)(2,1)} %param.20) | copy-start | bytes 5505028
  7.2 48.0 %all-gather.6.cloned.1.call-start = ((), (), s32[]{:S(2)}) async-start(), calls=%async_computation.4 | async-start | bytes 5308416 | tf_op jit(solution)/shard_map/all_gather | solution.py:65
  9.6 200.4 %copy-start.2 = (bf16[64,576]{1,0:T(8,128)(2,1)S(1)}, bf16[64,576]{1,0:T(8,128)(2,1)}, u32[]{:S(2)}) copy-start(bf16[64,576]{1,0:T(8,128)(2,1)} %param.16) | copy-start | bytes 221188
  9.6 200.4 %all-gather.4.cloned.1.call-start = ((), (), s32[]{:S(2)}) async-start(), calls=%async_computation.3 | async-start | bytes 5324800 | tf_op jit(solution)/shard_map/all_gather | solution.py:79
  210.0 5.8 copy-start.6
  220.0 22.8 %all-to-all-start.2 = ((f32[64,64,1]{0,2,1:T(1,128)}), f32[64,64,1]{0,2,1:T(1,128)S(1)}, u32[]{:S(2)}, u32[]{:S(2)}) async-start(f32[64,64,1]{0,2,1:T(1,128)} %copy.54), calls=%async_computation.2 | async-start | bytes 65536 | tf_op jit(solution)/shard_map/all_to_all | solution.py:108
  242.8 19.1 %all-to-all-start = ((f32[64,64,1]{0,2,1:T(1,128)}), f32[64,64,1]{0,2,1:T(1,128)S(1)}, u32[]{:S(2)}, u32[]{:S(2)}) async-start(f32[64,64,1]{0,2,1:T(1,128)} %copy.52), calls=%async_computation | async-start | bytes 65536 | tf_op jit(solution)/shard_map/all_to_all | solution.py:107
  261.9 183.9 %all-to-all-start.1 = ((bf16[64,64,512]{2,0,1:T(8,128)(2,1)}), bf16[64,64,512]{2,0,1:T(8,128)(2,1)}, u32[]{:S(2)}, u32[]{:S(2)}) async-start(bf16[64,64,512]{2,0,1:T(8,128)(2,1)} %copy.53), calls=%async_computation.1 | async-start | bytes 8388608 | tf_op jit(solution)/shard_map/all_to_all | solution.py:103
  269.3 183.2 %copy-start.1 = (bf16[1,512,128]{2,1,0:T(8,128)(2,1)S(1)}, bf16[1,512,128]{2,1,0:T(8,128)(2,1)}, u32[]{:S(2)}) copy-start(bf16[1,512,128]{2,1,0:T(8,128)(2,1)} %param.19) | copy-start | bytes 393220
  269.3 458.6 %all-reduce.3.cloned.1.call-start = ((), (), s32[]{:S(2)}) async-start(), calls=%async_computation.5 | async-start | bytes 3670016
  445.8 8.6 %copy-start.5 = (s32[64,8]{0,1:T(8,128)S(1)}, s32[64,8]{0,1:T(8,128)}, u32[]{:S(2)}) copy-start(s32[64,8]{0,1:T(8,128)} %param.23) | copy-start | bytes 6148
  452.5 275.4 %copy-start.4 = (bf16[1,7168]{1,0:T(2,128)(2,1)S(1)}, bf16[1,7168]{1,0:T(2,128)(2,1)}, u32[]{:S(2)}) copy-start(bf16[1,7168]{1,0:T(2,128)(2,1)} %param.21) | copy-start | bytes 43012
  452.5 278.4 %copy-start.3 = (f32[7168]{0:T(1024)S(1)}, f32[7168]{0:T(1024)}, u32[]{:S(2)}) copy-start(f32[7168]{0:T(1024)} %param.22) | copy-start | bytes 86020
Sparse Core Ops, SparseCore 0:
  10.1 44.9 all-gather.5
  58.7 151.2 all-gather.3
  454.5 273.3 all-reduce.2
where the time goes:
time: 840 us; the launch traced here: 839 us
  waiting for transfers between devices  661 us (79%)
  blocking collectives  100 us (12%)
  matrix products  26.8 us (3%)
  starting transfers between devices  20.6 us (2%)
  between operations  14.7 us (2%)
  local copies, waits for them, and re-layouts  10.4 us (1%)
    unnamed x4, waiting for transfers between devices  272 us
    all_to_all x1, waiting for transfers between devices, on_device(): lax.all_to_all(mixed, 'exp', split_axis=1, concat_axis=0, tiled=True)  176 us
    all_gather x1, waiting for transfers between devices, on_device(): queries = lax.all_gather(absorbed, 'exp', axis=1, tiled=True)  151 us
    all_gather x1, blocking collectives, on_device(): lax.all_gather(normalize(hidden, ffn_gain), 'exp', axis=0, tiled=True)  100 us
    all_gather x1, waiting for transfers between devices, on_device(): whole = lax.all_gather(flat_cache, 'ctx', axis=0, tiled=True)  40.8 us
  transfers between devices with their start and end apart: 6, of which 6 were waited for; matrix products, arithmetic and copies ran while one was open for 2% of the time, Pallas kernels for 0%

commit v1 on v0

v1 whole, which is shorter than its diff:
```python
import math

import jax
import jax.numpy as jnp
import numpy as np
from jax import lax
from jax.experimental import pallas as pl
from jax.experimental.pallas import tpu as pltpu
from jax.sharding import PartitionSpec as P

MESH = pl.DeviceIdType.MESH
F32 = jnp.float32
BF16 = jnp.bfloat16
N_CTX, N_EXP, N_X, N_Z = 8, 64, 4, 16
ROWS, LLOC, LAT, KVL, NOPE, RD, VD = 64, 8, 576, 512, 128, 64, 128
QL, D, CAP = 1536, 7168, 4
QW = NOPE + RD
COLS = D // 8
LANES = D // 128
SCALE = 1.0 / math.sqrt(QW)


def dot(a, b, ca=1, cb=0):
    return lax.dot_general(a, b, (((ca,), (cb,)), ((), ())), preferred_element_type=F32)


def send(src, dst, send_sem, recv_sem, device):
    pltpu.make_async_remote_copy(
        src_ref=src,
        dst_ref=dst,
        send_sem=send_sem,
        recv_sem=recv_sem,
        device_id=device,
        device_id_type=MESH,
    ).start()


def drain(ref, sem):
    pltpu.make_async_copy(ref, ref, sem).wait()


def each(low, high, body):
    def step(k, carry):
        body(k)
        return carry

    lax.fori_loop(low, high, step, 0)


def kernel(
    owner_s,
    lens_s,
    owner_g,
    owner_row,
    lens_g,
    freqs,
    ids,
    residual,
    gain,
    cache_hbm,
    ql_hbm,
    nl_hbm,
    wq_hbm,
    wk_hbm,
    wv_hbm,
    wo_hbm,
    hidden_ref,
    expert_ref,
    ql,
    wq,
    wk,
    wv,
    kbuf,
    qall,
    nlall,
    qsend,
    qrecv,
    lsend,
    lrecv,
    hall,
    wbuf,
    psend,
    precv,
    rsend,
    rrecv,
    flat,
    nbuf,
    idx_v,
    idx_s,
    load_sem,
    own_sem,
    send_sem,
    recv_sem,
    z_sem,
):
    c = lax.axis_index("ctx")
    e = lax.axis_index("exp")
    y, core = c // 2, lax.rem(c, 2)
    z, x = e // N_X, lax.rem(e, N_X)

    loads = [
        pltpu.make_async_copy(src, dst, load_sem.at[i])
        for i, (src, dst) in enumerate(
            [
                (ql_hbm, ql),
                (wq_hbm, wq),
                (wk_hbm, wk),
                (wv_hbm, wv),
                (nl_hbm, nlall.at[c]),
            ]
        )
    ]
    for load in loads:
        load.start()

    barrier = pltpu.get_barrier_semaphore()

    def greet(device):
        pl.semaphore_signal(barrier, inc=1, device_id=device, device_id_type=MESH)

    each(1, N_EXP, lambda k: greet((c, lax.rem(e + k, N_EXP))))

    def greet_plane(k):
        for i in range(N_X):
            greet((lax.rem(c + k, N_CTX), z * N_X + i))

    each(1, N_CTX, greet_plane)

    loads[0].wait()
    loads[1].wait()
    qall[c] = dot(ql[...], wq[...], 1, 1).astype(BF16)
    loads[4].wait()

    pl.semaphore_wait(barrier, N_EXP - 1 + (N_CTX - 1) * N_X)

    def send_q(k):
        to = (lax.rem(c + k, N_CTX), e)
        send(qall.at[c], qall.at[c], send_sem.at[0], recv_sem.at[0], to)

    each(1, N_CTX, send_q)

    own = pltpu.make_async_copy(cache_hbm.at[e], kbuf.at[e], recv_sem.at[1])
    own.start()

    def send_cache(k):
        j = lax.rem(e + k, N_EXP)
        send(cache_hbm.at[j], kbuf.at[e], send_sem.at[1], recv_sem.at[1], (c, j))

    each(1, N_EXP, send_cache)

    def send_new(k):
        to = (lax.rem(c + k, N_CTX), e)
        send(nlall.at[c], nlall.at[c], send_sem.at[2], recv_sem.at[2], to)

    each(1, N_CTX, send_new)

    def columns(i):
        return wo_hbm.at[:, pl.ds(pl.multiple_of((i * 2 + core) * COLS, 128), COLS)]

    own_w = pltpu.make_async_copy(columns(x), wbuf.at[x], own_sem)
    own_w.start()

    def send_w(k):
        i = lax.rem(x + k, N_X)
        send(columns(i), wbuf.at[x], send_sem.at[3], recv_sem.at[3], (c, z * N_X + i))

    each(1, N_X, send_w)

    names = ids[...]
    row = lax.broadcasted_iota(jnp.int32, (8, ROWS), 0)
    named = jnp.zeros((8, ROWS), F32)
    for i in range(4):
        hit = jnp.sum((names == e * 4 + i).astype(F32), 0, keepdims=True)
        named = jnp.where(row == i, hit, named)
    earlier = (
        lax.broadcasted_iota(jnp.int32, (ROWS, ROWS), 0)
        < lax.broadcasted_iota(jnp.int32, (ROWS, ROWS), 1)
    ).astype(F32)
    before = dot(named.astype(BF16), earlier.astype(BF16))
    number = lax.broadcasted_iota(jnp.int32, (8, ROWS), 1).astype(F32) + 1.0
    lane = lax.broadcasted_iota(jnp.int32, (8, 128), 1)
    chosen = jnp.zeros((8, 128), F32)
    for s in range(CAP):
        taken = jnp.where((before == s) & (named > 0.5), number, 0.0)
        chosen = jnp.where(lane == s, jnp.sum(taken, 1, keepdims=True), chosen)
    idx_v[...] = chosen.astype(jnp.int32)
    to_scalar = pltpu.make_async_copy(idx_v, idx_s, load_sem.at[5])
    to_scalar.start()

    mine = owner_g[pl.ds(c, 1), :]
    place = (lax.broadcasted_iota(jnp.int32, (N_CTX * ROWS, ROWS), 0) == mine).astype(F32)
    lengths = lens_g[pl.ds(c, 1), :].astype(F32)
    eye = lax.broadcasted_iota(jnp.int32, (ROWS, ROWS), 0) == lax.broadcasted_iota(
        jnp.int32, (ROWS, ROWS), 1
    )
    angles = jnp.sum(jnp.where(eye, lengths, 0.0), 1, keepdims=True) * freqs[...]
    cosines, sines = jnp.cos(angles), jnp.sin(angles)
    loads[2].wait()
    drain(qall.at[pl.ds(0, N_CTX - 1)], recv_sem.at[0])
    q = dot(place.astype(BF16), qall[...].reshape(N_CTX * ROWS, QW), 0, 0)
    absorbed = dot(q[:, :NOPE].astype(BF16), wk[...])
    first, second = q[:, NOPE : NOPE + RD // 2], q[:, NOPE + RD // 2 :]
    turned = jnp.concatenate(
        [first * cosines - second * sines, first * sines + second * cosines], 1
    )
    qsend[:, 0, :KVL] = absorbed.astype(BF16).astype(F32)
    qsend[:, 0, KVL:] = turned.astype(BF16).astype(F32)
    qrecv[e] = qsend[e]

    def send_query(k):
        j = lax.rem(e + k, N_EXP)
        send(qsend.at[j], qrecv.at[e], send_sem.at[4], recv_sem.at[4], (c, j))

    each(1, N_EXP, send_query)

    request = c * ROWS + e
    length = lens_s[request]
    slot = owner_s[request]
    drain(nlall.at[pl.ds(0, N_CTX - 1)], recv_sem.at[2])
    pick = (lax.broadcasted_iota(jnp.int32, (16, N_CTX * ROWS), 1) == slot).astype(F32)
    new = dot(pick.astype(BF16), nlall[...].reshape(N_CTX * ROWS, LAT))[0:1, :]
    drain(qrecv.at[pl.ds(0, N_EXP - 1)], recv_sem.at[4])
    queries = qrecv[:, 0, :]
    new_scores = jnp.sum(queries * new, 1, keepdims=True) * SCALE
    queries = queries.astype(BF16)
    drain(kbuf, recv_sem.at[1])
    keys = kbuf[...].astype(F32).reshape(N_EXP * LLOC, LAT).astype(BF16)
    scores = dot(queries, keys, 1, 1) * SCALE
    valid = lax.broadcasted_iota(jnp.int32, scores.shape, 1) < length
    top = jnp.max(jnp.where(valid, scores, -1e30), 1, keepdims=True)
    top = jnp.maximum(top, new_scores)
    weights = jnp.where(valid, jnp.exp(scores - top), 0.0)
    new_weight = jnp.exp(new_scores - top)
    total = jnp.sum(weights, 1, keepdims=True) + new_weight
    mixed = dot(weights.astype(BF16), keys[:, :KVL])
    mixed = mixed + new_weight.astype(BF16).astype(F32) * new[:, :KVL]
    lsend[:, 0, :] = (mixed / total).astype(BF16).astype(F32)
    lrecv[e] = lsend[e]

    def send_latent(k):
        j = lax.rem(e + k, N_EXP)
        send(lsend.at[j], lrecv.at[e], send_sem.at[5], recv_sem.at[5], (c, j))

    each(1, N_EXP, send_latent)

    loads[3].wait()
    drain(lrecv.at[pl.ds(0, N_EXP - 1)], recv_sem.at[5])
    at = c * N_X + x
    hall[at] = dot(lrecv[:, 0, :].astype(BF16), wv[...]).astype(BF16)

    def send_heads(k):
        to_c = lax.rem(c + k, N_CTX)
        for i in range(N_X):
            to_x = lax.rem(x + i, N_X)
            send(hall.at[at], hall.at[at], send_sem.at[6], recv_sem.at[6], (to_c, z * N_X + to_x))

    def send_heads_x(k):
        to_x = lax.rem(x + k, N_X)
        send(hall.at[at], hall.at[at], send_sem.at[6], recv_sem.at[6], (c, z * N_X + to_x))

    each(1, N_CTX, send_heads)
    each(1, N_X, send_heads_x)

    order = lax.broadcasted_iota(jnp.int32, (2 * ROWS, N_CTX * ROWS), 0)
    rest = order % 8
    wanted = (y * 2 + rest // N_X) * ROWS + (order // 8) * N_X + rest % N_X
    place = (owner_row[...] == wanted).astype(F32).astype(BF16)
    own_w.wait()
    drain(wbuf.at[pl.ds(0, N_X - 1)], recv_sem.at[3])
    drain(hall.at[pl.ds(0, N_CTX * N_X - 1)], recv_sem.at[6])
    partial = jnp.zeros((2 * ROWS, COLS), F32)
    heads = hall[...].reshape(N_CTX, N_X, ROWS, VD)
    for i in range(N_X):
        head = dot(place, heads[:, i].reshape(N_CTX * ROWS, VD)).astype(BF16)
        partial = partial + dot(head, wbuf[i])
    psend[...] = partial.reshape(N_Z, 8, COLS)
    precv[z] = psend[z]

    def send_partial(k):
        to_z = lax.rem(z + k, N_Z)
        send(psend.at[to_z], precv.at[z], send_sem.at[7], recv_sem.at[7], (c, to_z * N_X + x))

    each(1, N_Z, send_partial)
    drain(precv.at[pl.ds(0, N_Z - 1)], recv_sem.at[7])
    summed = precv[0]
    for i in range(1, N_Z):
        summed = summed + precv[i]

    rsend[:, 0, :] = summed
    mine_row, block = core * N_X + x, x * 2 + core
    rrecv[block] = rsend[mine_row]

    def send_row(k):
        j = lax.rem(mine_row + k, 8)
        to = (y * 2 + j // N_X, z * N_X + lax.rem(j, N_X))
        send(rsend.at[j], rrecv.at[block], send_sem.at[8], recv_sem.at[8], to)

    each(1, 8, send_row)
    drain(rrecv.at[pl.ds(0, 7)], recv_sem.at[8])
    hidden = residual[...].astype(F32) + rrecv[:, 0, :]
    hidden_ref[...] = hidden.astype(BF16)
    square = jnp.sum(jnp.sum(hidden * hidden, 1, keepdims=True), 0, keepdims=True)
    normed = hidden * lax.rsqrt(square * (1.0 / D) + 1e-06) * gain[...]
    for i in range(COLS // 128):
        flat[pl.ds(i, 8, stride=COLS // 128), :] = normed[:, i * 128 : (i + 1) * 128]
    nbuf[e] = flat[0:LANES, :].astype(BF16)

    def send_z(k):
        to_z = lax.rem(z + k, N_Z)
        send(nbuf.at[e], nbuf.at[e], send_sem.at[9], z_sem.at[z], (c, to_z * N_X + x))

    each(1, N_Z, send_z)

    def forward(k):
        from_z = lax.rem(z + N_Z - k, N_Z)
        at_row = from_z * N_X + x

        @pl.when(k > 0)
        def _():
            drain(nbuf.at[at_row], z_sem.at[from_z])

        for i in range(1, N_X):
            to_x = lax.rem(x + i, N_X)
            send(
                nbuf.at[at_row], nbuf.at[at_row], send_sem.at[10], recv_sem.at[9], (c, z * N_X + to_x)
            )

    each(0, N_Z, forward)
    to_scalar.wait()
    drain(nbuf.at[pl.ds(0, N_Z * (N_X - 1))], recv_sem.at[9])
    for i in range(4):
        for s in range(CAP):
            found = idx_s[i, s]
            rows = nbuf[jnp.clip(found - 1, 0, N_EXP - 1)].astype(F32)
            expert_ref[i * CAP + s] = jnp.where(found > 0, rows, 0.0).astype(BF16)

    drain(qall.at[pl.ds(0, N_CTX - 1)], send_sem.at[0])
    drain(kbuf.at[pl.ds(0, N_EXP - 1)], send_sem.at[1])
    drain(nlall.at[pl.ds(0, N_CTX - 1)], send_sem.at[2])
    drain(wbuf.at[pl.ds(0, N_X - 1)], send_sem.at[3])
    drain(qsend.at[pl.ds(0, N_EXP - 1)], send_sem.at[4])
    drain(lsend.at[pl.ds(0, N_EXP - 1)], send_sem.at[5])
    drain(hall.at[pl.ds(0, N_CTX * N_X - 1)], send_sem.at[6])
    drain(psend.at[pl.ds(0, N_Z - 1)], send_sem.at[7])
    drain(rsend.at[pl.ds(0, 7)], send_sem.at[8])
    drain(nbuf.at[pl.ds(0, N_Z - 1)], send_sem.at[9])
    drain(nbuf.at[pl.ds(0, N_Z * (N_X - 1))], send_sem.at[10])


def on_device(
    prefill_cache,
    owner_slot,
    cached_len,
    query_latent,
    new_latent,
    wq_up,
    wk_up,
    wv_up,
    w_out,
    residual,
    ffn_gain,
    expert_ids,
):
    half = (10000.0 ** (-2.0 * np.arange(RD // 2, dtype=np.float32) / RD)).astype(np.float32)
    smem = pl.BlockSpec(memory_space=pltpu.SMEM)
    vmem = pl.BlockSpec(memory_space=pltpu.VMEM)
    anywhere = pl.BlockSpec(memory_space=pl.ANY)
    hidden, expert_in = pl.pallas_call(
        kernel,
        out_shape=(
            jax.ShapeDtypeStruct((8, COLS), BF16),
            jax.ShapeDtypeStruct((4 * CAP, LANES, 128), BF16),
        ),
        in_specs=[smem] * 2 + [vmem] * 7 + [anywhere] * 7,
        out_specs=(vmem, vmem),
        scratch_shapes=[
            pltpu.VMEM((ROWS, QL), BF16),
            pltpu.VMEM((QW, QL), BF16),
            pltpu.VMEM((NOPE, KVL), BF16),
            pltpu.VMEM((KVL, VD), BF16),
            pltpu.VMEM((N_EXP, LLOC, LAT), BF16),
            pltpu.VMEM((N_CTX, ROWS, QW), BF16),
            pltpu.VMEM((N_CTX, ROWS, LAT), BF16),
            pltpu.VMEM((ROWS, 1, LAT), F32),
            pltpu.VMEM((N_EXP, 1, LAT), F32),
            pltpu.VMEM((N_EXP, 1, KVL), F32),
            pltpu.VMEM((ROWS, 1, KVL), F32),
            pltpu.VMEM((N_CTX * N_X, ROWS, VD), BF16),
            pltpu.VMEM((N_X, VD, COLS), BF16),
            pltpu.VMEM((N_Z, 8, COLS), F32),
            pltpu.VMEM((N_Z, 8, COLS), F32),
            pltpu.VMEM((8, 1, COLS), F32),
            pltpu.VMEM((8, 1, COLS), F32),
            pltpu.VMEM((64, 128), F32),
            pltpu.VMEM((N_EXP, LANES, 128), BF16),
            pltpu.VMEM((8, 128), jnp.int32),
            pltpu.SMEM((8, 128), jnp.int32),
            pltpu.SemaphoreType.DMA((6,)),
            pltpu.SemaphoreType.DMA,
            pltpu.SemaphoreType.DMA((11,)),
            pltpu.SemaphoreType.DMA((10,)),
            pltpu.SemaphoreType.DMA((N_Z,)),
        ],
        compiler_params=pltpu.CompilerParams(
            collective_id=0, has_side_effects=True, vmem_limit_bytes=60 * 1024 * 1024
        ),
        cost_estimate=pl.CostEstimate(
            flops=600_000_000, bytes_accessed=8_000_000, transcendentals=40_000
        ),
    )(
        owner_slot,
        cached_len,
        owner_slot.reshape(N_CTX, ROWS),
        owner_slot.reshape(1, N_CTX * ROWS),
        cached_len.reshape(N_CTX, ROWS),
        jnp.asarray(half).reshape(1, RD // 2),
        expert_ids.T,
        residual.reshape(8, COLS),
        ffn_gain.reshape(8, COLS),
        prefill_cache,
        query_latent,
        new_latent,
        wq_up.reshape(QL, QW).T,
        wk_up.reshape(NOPE, KVL),
        wv_up.reshape(KVL, VD),
        w_out,
    )
    return hidden.reshape(1, D), expert_in.reshape(1, 4, CAP, D)


def solution(mesh):
    placed = (
        P("ctx", "exp", None),
        P(),
        P(),
        P("ctx", None),
        P("ctx", None),
        P(None, "exp", None),
        P("exp", None, None),
        P("exp", None, None),
        P("exp", None),
        P(("ctx", "exp"), None),
        P(),
        P("ctx", None),
    )
    return jax.shard_map(
        on_device,
        mesh=mesh,
        in_specs=placed,
        out_specs=(P(("ctx", "exp"), None), P("ctx", "exp", None, None)),
        check_vma=False,
    )
```

time: 840 us -> 137 us (0.16)
  the two profiles are of different devices: /device:TPU:16 before, /device:TPU:1 now
where the time goes in v1:
time: 137 us; the launch traced here: 136 us
  Pallas kernels  127 us (93%)
  local copies, waits for them, and re-layouts  7.72 us (6%)
    pallas_call x1, Pallas kernels, on_device(): pl.pallas_call(kernel, out_shape=(jax.ShapeDtypeStruct((8, COLS), BF16),...  127 us

profile of v1, /device:TPU:1, one launch (start us, length us, event | category | flops | bytes accessed | tf_op | source)
XLA Modules:
  0.0 136.0 jit_solution(16197542677782829740)
XLA Ops:
  0.6 0.8 reduce
  1.5 0.6 reshape.41.residual
  2.1 1.4 %reshape.42.gain = f32[8,896]{1,0:T(8,128)} reshape(f32[7168]{0:T(1024)} %param.23) | data formatting | bytes 57344 | tf_op jit(solution)/shard_map/reshape | solution.py:419
  3.5 1.3 reshape.37.owner_g
  4.8 1.3 reshape.39.lens_g
  6.2 126.8 %shard_map.140 = (bf16[8,896]{1,0:T(8,128)(2,1)}, bf16[16,56,128]{2,1,0:T(8,128)(2,1)}) custom-call(s32[512]{0:T(512)} %owner_s.1, s32[512]{0:T(512)} %lens_s.1, s32[8,64]{1,0:T(8,128)} %reshape.37.owner_g, s32[1,512]{1,0:T(1,128)} %bitcast.14, s32[8,64]{1,0:T(8,128)} %reshape.39.lens_g, f32[1,32]{1,0:T(1,128)} %constant.8.freqs, s32[8,64]{1,0:T(8,128)} %bitcast.16, ...), custom_call_target="tpu_custom_call" | custom-call | flops 600000000 | bytes 8000000 | tf_op jit(solution)/shard_map/pallas_call | solution.py:368
  132.9 1.7 %reshape.47 = bf16[1,4,4,7168]{3,2,1,0:T(4,128)(2,1)} reshape(bf16[16,56,128]{2,1,0:T(8,128)(2,1)} %get-tuple-element.5) | data formatting | bytes 458752 | tf_op jit(solution)/shard_map/reshape | solution.py:428
  134.6 1.3 copy.15

commit v2 on v1

v2 whole, which is shorter than its diff:
```python
import math

import jax
import jax.numpy as jnp
import numpy as np
from jax import lax
from jax.experimental import pallas as pl
from jax.experimental.pallas import tpu as pltpu
from jax.sharding import PartitionSpec as P

MESH = pl.DeviceIdType.MESH
F32 = jnp.float32
BF16 = jnp.bfloat16
N_CTX, N_EXP, N_X, N_Z = 8, 64, 4, 16
ROWS, LLOC, LAT, KVL, NOPE, RD, VD = 64, 8, 576, 512, 128, 64, 128
QL, D, CAP = 1536, 7168, 4
QW = NOPE + RD
COLS = D // 8
PAIRS, NEAR = ROWS // 2, N_Z // 2
SCALE = 1.0 / math.sqrt(QW)


def dot(a, b, ca=1, cb=0):
    return lax.dot_general(a, b, (((ca,), (cb,)), ((), ())), preferred_element_type=F32)


def send(src, dst, send_sem, recv_sem, device):
    pltpu.make_async_remote_copy(
        src_ref=src,
        dst_ref=dst,
        send_sem=send_sem,
        recv_sem=recv_sem,
        device_id=device,
        device_id_type=MESH,
    ).start()


def drain(ref, sem):
    pltpu.make_async_copy(ref, ref, sem).wait()


def each(low, high, body):
    def step(k, carry):
        body(k)
        return carry

    lax.fori_loop(low, high, step, 0)


def offset(i, size):
    far = size // 2 - i // 2
    return jnp.where(i % 2 == 0, far, size - far)


def split(value):
    high = value.astype(BF16).astype(F32)
    middle = (value - high).astype(BF16).astype(F32)
    return high, middle, value - high - middle


def own_part(row, y, core):
    part = row[:, 0:128]
    for i in range(1, N_CTX // 2):
        part = jnp.where(y == i, row[:, i * 128 : (i + 1) * 128], part)
    return jnp.where(core == 0, part[:, :ROWS], part[:, ROWS:])


def kernel(
    owner_s,
    lens_s,
    owner_row,
    lens_row,
    freqs,
    ids,
    residual,
    gain,
    cache_hbm,
    ql_hbm,
    nl_hbm,
    wq_hbm,
    wk_hbm,
    wv_hbm,
    wo_hbm,
    hidden_ref,
    expert_ref,
    ql,
    wq,
    wk,
    wv,
    kbuf,
    qall,
    nlall,
    qsend,
    qrecv,
    lsend,
    lrecv,
    hall,
    wbuf,
    psend,
    precv,
    rsend,
    resid,
    zbuf,
    gbuf,
    load_sem,
    own_sem,
    send_sem,
    recv_sem,
    z_sem,
):
    c = lax.axis_index("ctx")
    e = lax.axis_index("exp")
    y, core = c // 2, lax.rem(c, 2)
    z, x = e // N_X, lax.rem(e, N_X)

    loads = [
        pltpu.make_async_copy(src, dst, load_sem.at[i])
        for i, (src, dst) in enumerate(
            [
                (ql_hbm, ql),
                (wq_hbm, wq),
                (wk_hbm, wk),
                (wv_hbm, wv),
                (nl_hbm, nlall.at[c]),
            ]
        )
    ]
    for load in loads:
        load.start()

    barrier = pltpu.get_barrier_semaphore()
    sent, due = [], {}

    def track(name, ref, i):
        sent.append((ref, send_sem.at[i]))
        due[name] = (ref, recv_sem.at[i])

    def arrive(name):
        drain(*due.pop(name))

    def greet(device):
        pl.semaphore_signal(barrier, inc=1, device_id=device, device_id_type=MESH)

    each(1, N_EXP, lambda k: greet((c, lax.rem(e + k, N_EXP))))

    def greet_plane(k):
        for i in range(N_X):
            greet((lax.rem(c + k, N_CTX), z * N_X + i))

    each(1, N_CTX, greet_plane)

    loads[0].wait()
    loads[1].wait()
    qall[c] = dot(ql[...], wq[...], 1, 1).astype(BF16)
    loads[4].wait()

    pl.semaphore_wait(barrier, N_EXP - 1 + (N_CTX - 1) * N_X)

    def send_q(k):
        to = (lax.rem(c + offset(k, N_CTX), N_CTX), e)
        send(qall.at[c], qall.at[c], send_sem.at[0], recv_sem.at[0], to)

    each(1, N_CTX, send_q)
    track("q", qall.at[pl.ds(0, N_CTX - 1)], 0)

    pair = lax.rem(e, PAIRS)
    own = pltpu.make_async_copy(
        cache_hbm.at[pl.ds(2 * pair, 2)], kbuf.at[NEAR // 2 * N_X + x], recv_sem.at[1]
    )
    own.start()

    def send_cache(i):
        step = i // N_X
        near = NEAR // 2 - (step + 1) // 2
        away = jnp.where(step % 2 == 1, near, N_Z - near)
        away = jnp.where((step == 0) & (z % 2 == 0), NEAR // 2, away)
        to_z = lax.rem(z + away, N_Z)
        to_x = lax.rem(x + i + jnp.where(step == NEAR - 1, 1, 0), N_X)
        into = lax.rem(N_Z - away + NEAR // 2, NEAR) * N_X + x
        pairs = pl.ds(2 * (lax.rem(to_z, NEAR) * N_X + to_x), 2)
        send(cache_hbm.at[pairs], kbuf.at[into], send_sem.at[1], recv_sem.at[1], (c, to_z * N_X + to_x))

    each(0, PAIRS - 1, send_cache)
    sent.append((kbuf.at[pl.ds(0, PAIRS - 1)], send_sem.at[1]))
    due["cache"] = (kbuf, recv_sem.at[1])

    def send_new(k):
        to = (lax.rem(c + offset(k, N_CTX), N_CTX), e)
        send(nlall.at[c], nlall.at[c], send_sem.at[2], recv_sem.at[2], to)

    each(1, N_CTX, send_new)
    track("new", nlall.at[pl.ds(0, N_CTX - 1)], 2)

    mine_row, block = core * N_X + x, x * 2 + core
    for i in range(8):
        rsend[i] = residual[:, i * COLS : (i + 1) * COLS].astype(F32)
    resid[mine_row] = rsend[block]

    def send_residual(k):
        to_x, to_core = lax.rem(x + k // 2, N_X), lax.rem(core + k, 2)
        to = (y * 2 + to_core, z * N_X + to_x)
        send(rsend.at[to_x * 2 + to_core], resid.at[mine_row], send_sem.at[8], recv_sem.at[8], to)

    each(1, 8, send_residual)
    track("residual", resid.at[pl.ds(0, 7)], 8)

    names = ids[...]
    row = lax.broadcasted_iota(jnp.int32, (8, ROWS), 0)
    named = jnp.zeros((8, ROWS), F32)
    for i in range(4):
        hit = jnp.sum((names == e * 4 + i).astype(F32), 0, keepdims=True)
        named = jnp.where(row == i, hit, named)
    earlier = (
        lax.broadcasted_iota(jnp.int32, (ROWS, ROWS), 0)
        < lax.broadcasted_iota(jnp.int32, (ROWS, ROWS), 1)
    ).astype(F32)
    before = dot(named.astype(BF16), earlier.astype(BF16))
    column = lax.broadcasted_iota(jnp.int32, (24, ROWS), 1)
    line = lax.broadcasted_iota(jnp.int32, (24, ROWS), 0)
    selection = jnp.where((line == 4 * CAP) & (column == e), 1.0, 0.0)
    for i in range(4):
        for s in range(CAP):
            taken = jnp.where((before[i : i + 1] == s) & (named[i : i + 1] > 0.5), 1.0, 0.0)
            selection = jnp.where(line == i * CAP + s, taken, selection)
    stage = lax.broadcasted_iota(jnp.int32, (1, ROWS), 1) // N_X
    stage = jnp.where(stage == 0, z, z + N_Z - offset(stage, N_Z)) % N_Z
    held = stage * N_X + lax.broadcasted_iota(jnp.int32, (1, ROWS), 1) % N_X
    held = (lax.broadcasted_iota(jnp.int32, (ROWS, ROWS), 0) == held).astype(F32)
    selection = dot(selection.astype(BF16), held.astype(BF16)).astype(BF16)

    mine = own_part(owner_row[...], y, core)
    place = (lax.broadcasted_iota(jnp.int32, (N_CTX * ROWS, ROWS), 0) == mine).astype(F32)
    lengths = own_part(lens_row[...], y, core).astype(F32)
    eye = lax.broadcasted_iota(jnp.int32, (ROWS, ROWS), 0) == lax.broadcasted_iota(
        jnp.int32, (ROWS, ROWS), 1
    )
    angles = jnp.sum(jnp.where(eye, lengths, 0.0), 1, keepdims=True) * freqs[...]
    cosines, sines = jnp.cos(angles), jnp.sin(angles)
    loads[2].wait()
    arrive("q")
    q = dot(place.astype(BF16), qall[...].reshape(N_CTX * ROWS, QW), 0, 0)
    absorbed = dot(q[:, :NOPE].astype(BF16), wk[...])
    first, second = q[:, NOPE : NOPE + RD // 2], q[:, NOPE + RD // 2 :]
    turned = jnp.concatenate(
        [first * cosines - second * sines, first * sines + second * cosines], 1
    )
    absorbed = jnp.concatenate([absorbed, turned], 1).astype(BF16)
    qsend[...] = absorbed.reshape(PAIRS, 2, LAT)
    own_query = pltpu.make_async_copy(qsend.at[pair], qrecv.at[e], own_sem.at[1])
    own_query.start()
    due["own_query"] = (qrecv.at[e], own_sem.at[1])

    def send_query(k):
        j = lax.rem(e + offset(k, N_EXP), N_EXP)
        send(qsend.at[lax.rem(j, PAIRS)], qrecv.at[e], send_sem.at[4], recv_sem.at[4], (c, j))

    each(1, N_EXP, send_query)
    track("query", qrecv.at[pl.ds(0, N_EXP - 1)], 4)

    def columns(i):
        return wo_hbm.at[:, pl.ds(pl.multiple_of((i * 2 + core) * COLS, 128), COLS)]

    own_w = pltpu.make_async_copy(columns(x), wbuf.at[x], own_sem.at[0])
    own_w.start()
    due["own_w"] = (wbuf.at[x], own_sem.at[0])

    def send_w(k):
        i = lax.rem(x + k, N_X)
        send(columns(i), wbuf.at[x], send_sem.at[3], recv_sem.at[3], (c, z * N_X + i))

    each(1, N_X, send_w)
    track("w", wbuf.at[pl.ds(0, N_X - 1)], 3)

    first_request = c * ROWS + 2 * pair
    width = PAIRS * LLOC
    slot = lax.broadcasted_iota(jnp.int32, (1, width), 1) // LLOC
    from_z = z + slot // N_X + N_Z - NEAR // 2
    from_z = jnp.where((slot < N_X) & (z % 2 == 1), z + NEAR // 2, from_z) % N_Z
    position = (from_z * N_X + slot % N_X) * LLOC
    position = position + lax.broadcasted_iota(jnp.int32, (1, width), 1) % LLOC
    even = lax.broadcasted_iota(jnp.int32, (2 * N_EXP, 1), 0) % 2 == 0
    valid = position < jnp.where(even, lens_s[first_request], lens_s[first_request + 1])
    chosen = lax.broadcasted_iota(jnp.int32, (16, 1), 0)
    chosen = jnp.where(chosen == 0, owner_s[first_request], owner_s[first_request + 1])
    pick = (lax.broadcasted_iota(jnp.int32, (16, N_CTX * ROWS), 1) == chosen).astype(F32)
    arrive("new")
    new = dot(pick.astype(BF16), nlall[...].reshape(N_CTX * ROWS, LAT))
    arrive("own_query")
    arrive("query")
    queries = qrecv[...].reshape(2 * N_EXP, LAT)
    new_scores = dot(queries, new.astype(BF16), 1, 1) * SCALE
    new_scores = jnp.where(even, new_scores[:, 0:1], new_scores[:, 1:2])
    new_scores = jnp.where(e < PAIRS, new_scores, -1e30)
    arrive("cache")
    keys = [kbuf[:, t].astype(F32).reshape(width, LAT).astype(BF16) for t in range(2)]
    scores = jnp.where(even, dot(queries, keys[0], 1, 1), dot(queries, keys[1], 1, 1)) * SCALE
    top = jnp.max(jnp.where(valid, scores, -1e30), 1, keepdims=True)
    top = jnp.maximum(top, new_scores)
    weights = jnp.where(valid, jnp.exp(scores - top), 0.0)
    new_weight = jnp.where(e < PAIRS, jnp.exp(new_scores - top), 0.0)
    total = jnp.sum(weights, 1, keepdims=True) + new_weight
    mixed = dot(jnp.where(even, weights, 0.0).astype(BF16), keys[0][:, :KVL])
    mixed = mixed + dot(jnp.where(even, 0.0, weights).astype(BF16), keys[1][:, :KVL])
    mixed = mixed + new_weight.astype(BF16).astype(F32) * jnp.where(
        even, new[0:1, :KVL], new[1:2, :KVL]
    )
    some = total > 0.0
    divisor = jnp.where(some, total, 1.0)
    parts = split(jnp.where(some, top + jnp.log(divisor), -1e30))
    lane = lax.broadcasted_iota(jnp.int32, (2 * N_EXP, 128), 1)
    tail = jnp.zeros((2 * N_EXP, 128), F32)
    for i in range(3):
        tail = jnp.where(lane == i, parts[i], tail)
    latent = jnp.concatenate([mixed / divisor, tail], 1).astype(BF16)
    lsend[...] = latent.reshape(N_EXP, 2, KVL + 128)
    own_latent = pltpu.make_async_copy(lsend.at[e], lrecv.at[e], own_sem.at[2])
    own_latent.start()
    due["own_latent"] = (lrecv.at[e], own_sem.at[2])

    def send_latent(k):
        j = lax.rem(e + offset(k, N_EXP), N_EXP)
        send(lsend.at[j], lrecv.at[e], send_sem.at[5], recv_sem.at[5], (c, j))

    each(1, N_EXP, send_latent)
    track("latent", lrecv.at[pl.ds(0, N_EXP - 1)], 5)

    loads[3].wait()
    arrive("own_latent")
    arrive("latent")
    at = c * N_X + x
    halves = lrecv[...].reshape(2 * N_EXP, KVL + 128).astype(F32)
    sums = halves[:, KVL : KVL + 1] + halves[:, KVL + 1 : KVL + 2] + halves[:, KVL + 2 : KVL + 3]
    peak = jnp.maximum(sums[:ROWS], sums[ROWS:])
    low, high = jnp.exp(sums[:ROWS] - peak), jnp.exp(sums[ROWS:] - peak)
    latent = (low * halves[:ROWS, :KVL] + high * halves[ROWS:, :KVL]) / (low + high)
    hall[at] = dot(latent.astype(BF16), wv[...]).astype(BF16)

    def send_heads(k):
        to_c = lax.rem(c + offset(k, N_CTX), N_CTX)
        for i in range(N_X):
            to_x = lax.rem(x + i, N_X)
            send(hall.at[at], hall.at[at], send_sem.at[6], recv_sem.at[6], (to_c, z * N_X + to_x))

    def send_heads_x(k):
        to_x = lax.rem(x + k, N_X)
        send(hall.at[at], hall.at[at], send_sem.at[6], recv_sem.at[6], (c, z * N_X + to_x))

    each(1, N_CTX, send_heads)
    each(1, N_X, send_heads_x)
    track("heads", hall.at[pl.ds(0, N_CTX * N_X - 1)], 6)

    order = lax.broadcasted_iota(jnp.int32, (2 * ROWS, N_CTX * ROWS), 0)
    rest = order % 8
    wanted = (y * 2 + rest // N_X) * ROWS + (order // 8) * N_X + rest % N_X
    place = (owner_row[...] == wanted).astype(F32).astype(BF16)
    arrive("own_w")
    arrive("w")
    arrive("heads")
    partial = jnp.zeros((2 * ROWS, COLS), F32)
    heads = hall[...].reshape(N_CTX, N_X, ROWS, VD)
    for i in range(N_X):
        head = dot(place, heads[:, i].reshape(N_CTX * ROWS, VD)).astype(BF16)
        partial = partial + dot(head, wbuf[i])
    psend[...] = partial.reshape(N_Z, 8, COLS).astype(BF16)
    precv[z] = psend[z]

    def send_partial(k):
        to_z = lax.rem(z + offset(k, N_Z), N_Z)
        send(psend.at[to_z], precv.at[z], send_sem.at[7], recv_sem.at[7], (c, to_z * N_X + x))

    each(1, N_Z, send_partial)
    track("partial", precv.at[pl.ds(0, N_Z - 1)], 7)
    arrive("partial")
    summed = precv[0].astype(F32)
    for i in range(1, N_Z):
        summed = summed + precv[i].astype(F32)

    arrive("residual")
    hidden = (summed + resid[:, 0, :]).astype(BF16)
    zbuf[0] = hidden.reshape(2, N_X, COLS)

    def send_z(k):
        to_z = lax.rem(z + offset(k, N_Z), N_Z)
        send(zbuf.at[0], zbuf.at[k], send_sem.at[9], z_sem.at[k], (c, to_z * N_X + x))

    def spread(low, size):
        here = pl.ds(low, size)
        for k in range(1, 8):
            to_x, to_core = lax.rem(x + k // 2, N_X), lax.rem(core + k, 2)
            to = (y * 2 + to_core, z * N_X + to_x)
            send(zbuf.at[here, to_core], gbuf.at[block, here], send_sem.at[10], recv_sem.at[10], to)

    def landed(k):
        drain(zbuf.at[k], z_sem.at[k])

    each(1, 8, send_z)
    spread(0, 1)
    each(1, 4, landed)
    each(8, 12, send_z)
    spread(1, 3)
    each(4, 8, landed)
    each(12, 16, send_z)
    spread(4, 4)
    each(8, 12, landed)
    spread(8, 4)
    each(12, 16, landed)
    spread(12, 4)
    sent.append((zbuf.at[pl.ds(0, N_Z - 1)], send_sem.at[9]))
    track("rows", gbuf.at[pl.ds(0, 7)], 10)
    gbuf[block] = zbuf[:, core]
    arrive("rows")

    picked = []
    square = jnp.zeros((24, 1), F32)
    for i in range(8):
        rows = dot(selection, gbuf[i].reshape(ROWS, COLS))
        square = square + jnp.sum(rows * rows, 1, keepdims=True)
        picked.append(rows)
    factor = lax.rsqrt(square * (1.0 / D) + 1e-06)
    for i in range(8):
        there = slice(i * COLS, (i + 1) * COLS)
        hidden_ref[:, there] = picked[i][4 * CAP : 4 * CAP + 1].astype(BF16)
        expert_ref[:, there] = (picked[i] * factor * gain[:, there])[: 4 * CAP].astype(BF16)

    for ref, sem in sent:
        drain(ref, sem)


def on_device(
    prefill_cache,
    owner_slot,
    cached_len,
    query_latent,
    new_latent,
    wq_up,
    wk_up,
    wv_up,
    w_out,
    residual,
    ffn_gain,
    expert_ids,
):
    half = (10000.0 ** (-2.0 * np.arange(RD // 2, dtype=np.float32) / RD)).astype(np.float32)
    smem = pl.BlockSpec(memory_space=pltpu.SMEM)
    vmem = pl.BlockSpec(memory_space=pltpu.VMEM)
    anywhere = pl.BlockSpec(memory_space=pl.ANY)
    hidden, expert_in = pl.pallas_call(
        kernel,
        out_shape=(
            jax.ShapeDtypeStruct((1, D), BF16),
            jax.ShapeDtypeStruct((4 * CAP, D), BF16),
        ),
        in_specs=[smem] * 2 + [vmem] * 6 + [anywhere] * 7,
        out_specs=(vmem, vmem),
        scratch_shapes=[
            pltpu.VMEM((ROWS, QL), BF16),
            pltpu.VMEM((QW, QL), BF16),
            pltpu.VMEM((NOPE, KVL), BF16),
            pltpu.VMEM((KVL, VD), BF16),
            pltpu.VMEM((PAIRS, 2, LLOC, LAT), BF16),
            pltpu.VMEM((N_CTX, ROWS, QW), BF16),
            pltpu.VMEM((N_CTX, ROWS, LAT), BF16),
            pltpu.VMEM((PAIRS, 2, LAT), BF16),
            pltpu.VMEM((N_EXP, 2, LAT), BF16),
            pltpu.VMEM((N_EXP, 2, KVL + 128), BF16),
            pltpu.VMEM((N_EXP, 2, KVL + 128), BF16),
            pltpu.VMEM((N_CTX * N_X, ROWS, VD), BF16),
            pltpu.VMEM((N_X, VD, COLS), BF16),
            pltpu.VMEM((N_Z, 8, COLS), BF16),
            pltpu.VMEM((N_Z, 8, COLS), BF16),
            pltpu.VMEM((8, 1, COLS), F32),
            pltpu.VMEM((8, 1, COLS), F32),
            pltpu.VMEM((N_Z, 2, N_X, COLS), BF16),
            pltpu.VMEM((8, N_Z, N_X, COLS), BF16),
            pltpu.SemaphoreType.DMA((5,)),
            pltpu.SemaphoreType.DMA((3,)),
            pltpu.SemaphoreType.DMA((11,)),
            pltpu.SemaphoreType.DMA((11,)),
            pltpu.SemaphoreType.DMA((N_Z,)),
        ],
        compiler_params=pltpu.CompilerParams(
            collective_id=0, has_side_effects=True, vmem_limit_bytes=60 * 1024 * 1024
        ),
        cost_estimate=pl.CostEstimate(
            flops=600_000_000, bytes_accessed=8_000_000, transcendentals=40_000
        ),
    )(
        owner_slot,
        cached_len,
        owner_slot.reshape(1, N_CTX * ROWS),
        cached_len.reshape(1, N_CTX * ROWS),
        jnp.asarray(half).reshape(1, RD // 2),
        expert_ids.T,
        residual,
        ffn_gain.reshape(1, D),
        prefill_cache,
        query_latent,
        new_latent,
        wq_up.reshape(QL, QW).T,
        wk_up.reshape(NOPE, KVL),
        wv_up.reshape(KVL, VD),
        w_out,
    )
    return hidden, expert_in.reshape(1, 4, CAP, D)


def solution(mesh):
    placed = (
        P("ctx", "exp", None),
        P(),
        P(),
        P("ctx", None),
        P("ctx", None),
        P(None, "exp", None),
        P("exp", None, None),
        P("exp", None, None),
        P("exp", None),
        P(("ctx", "exp"), None),
        P(),
        P("ctx", None),
    )
    return jax.shard_map(
        on_device,
        mesh=mesh,
        in_specs=placed,
        out_specs=(P(("ctx", "exp"), None), P("ctx", "exp", None, None)),
        check_vma=False,
    )
```

time: 137 us -> 103 us (0.75)
  Pallas kernels: 127 us -> 99.3 us
  local copies, waits for them, and re-layouts: 7.72 us -> 3.1 us
    pallas_call x1, Pallas kernels: 127 us -> 99.3 us  [on_device(): pl.pallas_call(kernel, out_shape=(jax.ShapeDtypeStruct((1, D), BF16), jax...]
    reshape x5 -> x1, local copies, waits for them, and re-layouts: 6.38 us -> 1.72 us  [on_device(): return (hidden, expert_in.reshape(1, 4, CAP, D))]
where the time goes in v2:
time: 103 us
  Pallas kernels  99.3 us (96%)
  local copies, waits for them, and re-layouts  3.1 us (3%)
    pallas_call x1, Pallas kernels, on_device(): pl.pallas_call(kernel, out_shape=(jax.ShapeDtypeStruct((1, D), BF16), jax...  99.3 us

profile of v2, /device:TPU:1, one launch (start us, length us, event | category | flops | bytes accessed | tf_op | source)
XLA Modules:
  0.0 103.0 jit_solution(16143429048305713441)
XLA Ops:
  0.6 99.3 %shard_map.140 = (bf16[1,7168]{1,0:T(2,128)(2,1)}, bf16[16,7168]{1,0:T(8,128)(2,1)}) custom-call(s32[512]{0:T(512)} %owner_s.1, s32[512]{0:T(512)} %lens_s.1, s32[1,512]{1,0:T(1,128)} %bitcast.13, s32[1,512]{1,0:T(1,128)} %bitcast.14, f32[1,32]{1,0:T(1,128)} %constant.8.freqs, s32[8,64]{1,0:T(8,128)} %bitcast.15, bf16[1,7168]{1,0:T(2,128)(2,1)} %residual.1, ...), custom_call_target="tpu_custom_call" | custom-call | flops 600000000 | bytes 8000000 | tf_op jit(solution)/shard_map/pallas_call | solution.py:447
  99.9 1.7 %reshape.35 = bf16[1,4,4,7168]{3,2,1,0:T(4,128)(2,1)} reshape(bf16[16,7168]{1,0:T(8,128)(2,1)} %get-tuple-element.5) | data formatting | bytes 458752 | tf_op jit(solution)/shard_map/reshape | solution.py:504
  101.7 1.4 %copy.16 = bf16[1,7168]{1,0:T(2,128)(2,1)} copy(bf16[1,7168]{1,0:T(2,128)(2,1)} %get-tuple-element.8) | data formatting | bytes 28672

commit v3 on v2

--- a/solution.py
+++ b/solution.py
@@ -13,7 +13,7 @@
 BF16 = jnp.bfloat16
 N_CTX, N_EXP, N_X, N_Z = 8, 64, 4, 16
 ROWS, LLOC, LAT, KVL, NOPE, RD, VD = 64, 8, 576, 512, 128, 64, 128
-QL, D, CAP = 1536, 7168, 4
+QL, D, CAP, TOPK, SLOTS = 1536, 7168, 4, 8, 16
 QW = NOPE + RD
 COLS = D // 8
 PAIRS, NEAR = ROWS // 2, N_Z // 2
@@ -56,6 +56,10 @@
     high = value.astype(BF16).astype(F32)
     middle = (value - high).astype(BF16).astype(F32)
     return high, middle, value - high - middle
+
+
+def one_hot(mask):
+    return mask.astype(F32).astype(BF16)
 
 
 def own_part(row, y, core):
@@ -94,13 +98,21 @@
     qrecv,
     lsend,
     lrecv,
+    hsend,
     hall,
     wbuf,
     psend,
+    passed,
+    psum,
     precv,
     rsend,
     resid,
+    other_ids,
+    selection,
     zbuf,
+    osend,
+    orecv,
+    slots,
     gbuf,
     load_sem,
     own_sem,
@@ -184,6 +196,7 @@
     sent.append((kbuf.at[pl.ds(0, PAIRS - 1)], send_sem.at[1]))
     due["cache"] = (kbuf, recv_sem.at[1])
 
+
     def send_new(k):
         to = (lax.rem(c + offset(k, N_CTX), N_CTX), e)
         send(nlall.at[c], nlall.at[c], send_sem.at[2], recv_sem.at[2], to)
@@ -204,29 +217,8 @@
     each(1, 8, send_residual)
     track("residual", resid.at[pl.ds(0, 7)], 8)
 
-    names = ids[...]
-    row = lax.broadcasted_iota(jnp.int32, (8, ROWS), 0)
-    named = jnp.zeros((8, ROWS), F32)
-    for i in range(4):
-        hit = jnp.sum((names == e * 4 + i).astype(F32), 0, keepdims=True)
-        named = jnp.where(row == i, hit, named)
-    earlier = (
-        lax.broadcasted_iota(jnp.int32, (ROWS, ROWS), 0)
-        < lax.broadcasted_iota(jnp.int32, (ROWS, ROWS), 1)
-    ).astype(F32)
-    before = dot(named.astype(BF16), earlier.astype(BF16))
-    column = lax.broadcasted_iota(jnp.int32, (24, ROWS), 1)
-    line = lax.broadcasted_iota(jnp.int32, (24, ROWS), 0)
-    selection = jnp.where((line == 4 * CAP) & (column == e), 1.0, 0.0)
-    for i in range(4):
-        for s in range(CAP):
-            taken = jnp.where((before[i : i + 1] == s) & (named[i : i + 1] > 0.5), 1.0, 0.0)
-            selection = jnp.where(line == i * CAP + s, taken, selection)
-    stage = lax.broadcasted_iota(jnp.int32, (1, ROWS), 1) // N_X
-    stage = jnp.where(stage == 0, z, z + N_Z - offset(stage, N_Z)) % N_Z
-    held = stage * N_X + lax.broadcasted_iota(jnp.int32, (1, ROWS), 1) % N_X
-    held = (lax.broadcasted_iota(jnp.int32, (ROWS, ROWS), 0) == held).astype(F32)
-    selection = dot(selection.astype(BF16), held.astype(BF16)).astype(BF16)
+    send(ids, other_ids, send_sem.at[11], recv_sem.at[11], (y * 2 + 1 - core, e))
+    track("ids", other_ids, 11)
 
     mine = own_part(owner_row[...], y, core)
     place = (lax.broadcasted_iota(jnp.int32, (N_CTX * ROWS, ROWS), 0) == mine).astype(F32)
@@ -257,6 +249,7 @@
     each(1, N_EXP, send_query)
     track("query", qrecv.at[pl.ds(0, N_EXP - 1)], 4)
 
+
     def columns(i):
         return wo_hbm.at[:, pl.ds(pl.multiple_of((i * 2 + core) * COLS, 128), COLS)]
 
@@ -270,6 +263,28 @@
 
     each(1, N_X, send_w)
     track("w", wbuf.at[pl.ds(0, N_X - 1)], 3)
+
+    arrive("ids")
+    earlier = lax.broadcasted_iota(jnp.int32, (ROWS, ROWS), 0) < lax.broadcasted_iota(
+        jnp.int32, (ROWS, ROWS), 1
+    )
+    stage = lax.broadcasted_iota(jnp.int32, (1, ROWS), 1) // N_X
+    stage = jnp.where(stage == 0, z, z + N_Z - offset(stage, N_Z)) % N_Z
+    held = stage * N_X + lax.broadcasted_iota(jnp.int32, (1, ROWS), 1) % N_X
+    held = one_hot(lax.broadcasted_iota(jnp.int32, (ROWS, ROWS), 0) == held)
+    expert = z * 16 + lax.broadcasted_iota(jnp.int32, (16, ROWS), 0)
+    line = lax.broadcasted_iota(jnp.int32, (ROWS, 16), 0)
+    widen = one_hot(line // CAP == lax.broadcasted_iota(jnp.int32, (ROWS, 16), 1))
+    slot_of = (lax.broadcasted_iota(jnp.int32, (ROWS, ROWS), 0) % CAP).astype(F32)
+    for g in range(2):
+        names = jnp.where(core == g, ids[...], other_ids[...])
+        named = jnp.zeros((16, ROWS), F32)
+        for i in range(TOPK):
+            named = named + (names[i : i + 1] == expert).astype(F32)
+        named = named.astype(BF16)
+        before = dot(named, one_hot(earlier)).astype(BF16)
+        taken = (dot(widen, named) > 0.5) & (dot(widen, before) == slot_of)
+        selection[g] = dot(one_hot(taken), held).astype(BF16)
 
     first_request = c * ROWS + 2 * pair
     width = PAIRS * LLOC
@@ -324,6 +339,25 @@
     each(1, N_EXP, send_latent)
     track("latent", lrecv.at[pl.ds(0, N_EXP - 1)], 5)
 
+    def ranks(owner):
+        rows = jnp.sum(jnp.where(eye, owner, 0.0), 1, keepdims=True)
+        return jnp.sum(jnp.where((rows == owner) & earlier, 1.0, 0.0), 0, keepdims=True)
+
+    owner = (mine // ROWS).astype(F32)
+    key = (owner * SLOTS + ranks(owner)).astype(jnp.int32)
+    bucket = one_hot(lax.broadcasted_iota(jnp.int32, (N_CTX * SLOTS, ROWS), 0) == key)
+    keys = []
+    for i in range(N_CTX):
+        owner = owner_row[:, i * ROWS : (i + 1) * ROWS] // ROWS
+        key = (i * 2 + owner - 2 * y) * SLOTS + ranks(owner.astype(F32)).astype(jnp.int32)
+        keys.append(jnp.where(owner // 2 == y, key, -1))
+    keys = jnp.concatenate(keys, 1)
+    keys = one_hot(lax.broadcasted_iota(jnp.int32, (N_CTX * 2 * SLOTS, N_CTX * ROWS), 0) == keys)
+    order = lax.broadcasted_iota(jnp.int32, (2 * ROWS, N_CTX * ROWS), 0)
+    rest = order % 8
+    wanted = (y * 2 + rest // N_X) * ROWS + (order // 8) * N_X + rest % N_X
+    place = dot(one_hot(owner_row[...] == wanted), keys, 1, 1).astype(BF16)
+
     loads[3].wait()
     arrive("own_latent")
     arrive("latent")
@@ -333,97 +367,149 @@
     peak = jnp.maximum(sums[:ROWS], sums[ROWS:])
     low, high = jnp.exp(sums[:ROWS] - peak), jnp.exp(sums[ROWS:] - peak)
     latent = (low * halves[:ROWS, :KVL] + high * halves[ROWS:, :KVL]) / (low + high)
-    hall[at] = dot(latent.astype(BF16), wv[...]).astype(BF16)
+    value = dot(latent.astype(BF16), wv[...]).astype(BF16)
+    hsend[...] = dot(bucket, value).astype(BF16).reshape(N_CTX // 2, 2 * SLOTS, VD)
+    hall[at] = hsend[y]
 
     def send_heads(k):
         to_c = lax.rem(c + offset(k, N_CTX), N_CTX)
         for i in range(N_X):
-            to_x = lax.rem(x + i, N_X)
-            send(hall.at[at], hall.at[at], send_sem.at[6], recv_sem.at[6], (to_c, z * N_X + to_x))
+            to = (to_c, z * N_X + lax.rem(x + i, N_X))
+            send(hsend.at[to_c // 2], hall.at[at], send_sem.at[6], recv_sem.at[6], to)
 
     def send_heads_x(k):
-        to_x = lax.rem(x + k, N_X)
-        send(hall.at[at], hall.at[at], send_sem.at[6], recv_sem.at[6], (c, z * N_X + to_x))
+        to = (c, z * N_X + lax.rem(x + k, N_X))
+        send(hsend.at[y], hall.at[at], send_sem.at[6], recv_sem.at[6], to)
 
     each(1, N_CTX, send_heads)
     each(1, N_X, send_heads_x)
     track("heads", hall.at[pl.ds(0, N_CTX * N_X - 1)], 6)
 
-    order = lax.broadcasted_iota(jnp.int32, (2 * ROWS, N_CTX * ROWS), 0)
-    rest = order % 8
-    wanted = (y * 2 + rest // N_X) * ROWS + (order // 8) * N_X + rest % N_X
-    place = (owner_row[...] == wanted).astype(F32).astype(BF16)
     arrive("own_w")
     arrive("w")
     arrive("heads")
     partial = jnp.zeros((2 * ROWS, COLS), F32)
-    heads = hall[...].reshape(N_CTX, N_X, ROWS, VD)
+    heads = hall[...].reshape(N_CTX, N_X, 2 * SLOTS, VD)
     for i in range(N_X):
-        head = dot(place, heads[:, i].reshape(N_CTX * ROWS, VD)).astype(BF16)
+        head = dot(place, heads[:, i].reshape(N_CTX * 2 * SLOTS, VD)).astype(BF16)
         partial = partial + dot(head, wbuf[i])
     psend[...] = partial.reshape(N_Z, 8, COLS).astype(BF16)
-    precv[z] = psend[z]
-
-    def send_partial(k):
-        to_z = lax.rem(z + offset(k, N_Z), N_Z)
-        send(psend.at[to_z], precv.at[z], send_sem.at[7], recv_sem.at[7], (c, to_z * N_X + x))
-
-    each(1, N_Z, send_partial)
-    track("partial", precv.at[pl.ds(0, N_Z - 1)], 7)
+    precv[4] = psend[z]
+
+    def at_z(hop):
+        return lax.rem(z + hop + N_Z, N_Z)
+
+    def along_z(source, into, hop, recv):
+        send(source, into, send_sem.at[7], recv, (c, at_z(hop) * N_X + x))
+
+    for j in range(3):
+        along_z(psend.at[at_z(-5 - j)], passed.at[0, j], -1 - j, z_sem.at[0])
+        along_z(psend.at[at_z(5 + j)], passed.at[1, j], 1 + j, z_sem.at[1])
+
+    @pl.when(z % 2 == 0)
+    def _():
+        along_z(psend.at[at_z(8)], passed.at[0, 3], -4, z_sem.at[2])
+
+    @pl.when(z % 2 == 1)
+    def _():
+        along_z(psend.at[at_z(8)], passed.at[1, 3], 4, z_sem.at[2])
+
+    for j in range(1, 4):
+        along_z(psend.at[at_z(j)], precv.at[4 - j], j, recv_sem.at[7])
+        along_z(psend.at[at_z(-j)], precv.at[4 + j], -j, recv_sem.at[7])
+    for side in range(2):
+        drain(passed.at[side, pl.ds(0, 3)], z_sem.at[side])
+        hop = -4 if side == 0 else 4
+        through = psend[at_z(hop)].astype(F32)
+        for j in range(3):
+            through = through + passed[side, j].astype(F32)
+        psum[side] = through.astype(BF16)
+
+        @pl.when(z % 2 == side)
+        def _():
+            drain(passed.at[side, 3], z_sem.at[2])
+            psum[side] = (through + passed[side, 3].astype(F32)).astype(BF16)
+
+        along_z(psum.at[side], precv.at[4 - hop], hop, recv_sem.at[7])
+    sent.append((psend.at[pl.ds(0, N_Z - 1)], send_sem.at[7]))
+    due["partial"] = (precv.at[pl.ds(0, 8)], recv_sem.at[7])
     arrive("partial")
     summed = precv[0].astype(F32)
-    for i in range(1, N_Z):
+    for i in range(1, 9):
         summed = summed + precv[i].astype(F32)
 
     arrive("residual")
-    hidden = (summed + resid[:, 0, :]).astype(BF16)
-    zbuf[0] = hidden.reshape(2, N_X, COLS)
-
-    def send_z(k):
-        to_z = lax.rem(z + offset(k, N_Z), N_Z)
-        send(zbuf.at[0], zbuf.at[k], send_sem.at[9], z_sem.at[k], (c, to_z * N_X + x))
-
-    def spread(low, size):
-        here = pl.ds(low, size)
-        for k in range(1, 8):
-            to_x, to_core = lax.rem(x + k // 2, N_X), lax.rem(core + k, 2)
-            to = (y * 2 + to_core, z * N_X + to_x)
-            send(zbuf.at[here, to_core], gbuf.at[block, here], send_sem.at[10], recv_sem.at[10], to)
-
-    def landed(k):
-        drain(zbuf.at[k], z_sem.at[k])
-
-    each(1, 8, send_z)
-    spread(0, 1)
-    each(1, 4, landed)
-    each(8, 12, send_z)
-    spread(1, 3)
-    each(4, 8, landed)
-    each(12, 16, send_z)
-    spread(4, 4)
-    each(8, 12, landed)
-    spread(8, 4)
-    each(12, 16, landed)
-    spread(12, 4)
+    hidden = summed + resid[:, 0, :]
+    zbuf[0] = hidden.astype(BF16).reshape(2, N_X, COLS)
+
+    def pass_on(source, into, hop, recv):
+        send(zbuf.at[source], zbuf.at[into], send_sem.at[9], recv, (c, at_z(hop) * N_X + x))
+
+    pass_on(0, 8, 4, z_sem.at[3])
+    pass_on(0, 9, -4, z_sem.at[4])
+    for j in range(1, 4):
+        pass_on(0, 16 - 2 * j, j, recv_sem.at[9])
+        pass_on(0, 17 - 2 * j, -j, recv_sem.at[9])
+
+    osend[:, 0, :] = hidden
+    orecv[block] = osend[mine_row]
+
+    def send_row(k):
+        to_x, to_core = lax.rem(x + k // 2, N_X), lax.rem(core + k, 2)
+        to = (y * 2 + to_core, z * N_X + to_x)
+        send(osend.at[to_core * N_X + to_x], orecv.at[block], send_sem.at[12], recv_sem.at[12], to)
+
+    each(1, 8, send_row)
+    track("row", orecv.at[pl.ds(0, 7)], 12)
+
+    for side in range(2):
+        drain(zbuf.at[8 + side], z_sem.at[3 + side])
+        way = 1 - 2 * side
+
+        @pl.when(z % 2 == side)
+        def _():
+            pass_on(8 + side, 1, 4 * way, recv_sem.at[9])
+
+        for j in range(3):
+            pass_on(8 + side, 2 + 2 * j + side, (3 - j) * way, recv_sem.at[9])
     sent.append((zbuf.at[pl.ds(0, N_Z - 1)], send_sem.at[9]))
-    track("rows", gbuf.at[pl.ds(0, 7)], 10)
-    gbuf[block] = zbuf[:, core]
-    arrive("rows")
-
-    picked = []
-    square = jnp.zeros((24, 1), F32)
+    due["columns"] = (zbuf.at[pl.ds(0, N_Z - 3)], recv_sem.at[9])
+
+    arrive("columns")
+    for g in range(2):
+        rows = dot(selection[g], zbuf[:, g].reshape(ROWS, COLS)).astype(BF16)
+        slots[g] = rows.reshape(N_X, 16, COLS)
+
+    def send_slots(k):
+        to_x, to_core = lax.rem(x + k // 2, N_X), lax.rem(core + k, 2)
+        to = (y * 2 + to_core, z * N_X + to_x)
+        send(slots.at[to_core, to_x], gbuf.at[block], send_sem.at[10], recv_sem.at[10], to)
+
+    each(1, 8, send_slots)
+    track("slots", gbuf.at[pl.ds(0, 7)], 10)
+    gbuf[block] = slots[core, x]
+    arrive("row")
     for i in range(8):
-        rows = dot(selection, gbuf[i].reshape(ROWS, COLS))
+        hidden_ref[:, i * COLS : (i + 1) * COLS] = orecv[i].astype(BF16)
+    arrive("slots")
+
+    square = jnp.zeros((16, 1), F32)
+    for i in range(8):
+        rows = gbuf[i].astype(F32)
         square = square + jnp.sum(rows * rows, 1, keepdims=True)
-        picked.append(rows)
     factor = lax.rsqrt(square * (1.0 / D) + 1e-06)
     for i in range(8):
         there = slice(i * COLS, (i + 1) * COLS)
-        hidden_ref[:, there] = picked[i][4 * CAP : 4 * CAP + 1].astype(BF16)
-        expert_ref[:, there] = (picked[i] * factor * gain[:, there])[: 4 * CAP].astype(BF16)
+        expert_ref[:, there] = (gbuf[i].astype(F32) * factor * gain[:, there]).astype(BF16)
 
     for ref, sem in sent:
         drain(ref, sem)
+
+
+def place_results(hidden, expert_in, hidden_ref, expert_ref):
+    hidden_ref[...] = hidden[...]
+    for i in range(4):
+        expert_ref[0, i] = expert_in[i * CAP : (i + 1) * CAP]
 
 
 def on_device(
@@ -464,19 +550,27 @@
             pltpu.VMEM((N_EXP, 2, LAT), BF16),
             pltpu.VMEM((N_EXP, 2, KVL + 128), BF16),
             pltpu.VMEM((N_EXP, 2, KVL + 128), BF16),
-            pltpu.VMEM((N_CTX * N_X, ROWS, VD), BF16),
+            pltpu.VMEM((N_CTX // 2, 2 * SLOTS, VD), BF16),
+            pltpu.VMEM((N_CTX * N_X, 2 * SLOTS, VD), BF16),
             pltpu.VMEM((N_X, VD, COLS), BF16),
             pltpu.VMEM((N_Z, 8, COLS), BF16),
-            pltpu.VMEM((N_Z, 8, COLS), BF16),
+            pltpu.VMEM((2, 4, 8, COLS), BF16),
+            pltpu.VMEM((2, 8, COLS), BF16),
+            pltpu.VMEM((9, 8, COLS), BF16),
             pltpu.VMEM((8, 1, COLS), F32),
             pltpu.VMEM((8, 1, COLS), F32),
+            pltpu.VMEM((TOPK, ROWS), jnp.int32),
+            pltpu.VMEM((2, ROWS, ROWS), BF16),
             pltpu.VMEM((N_Z, 2, N_X, COLS), BF16),
-            pltpu.VMEM((8, N_Z, N_X, COLS), BF16),
+            pltpu.VMEM((8, 1, COLS), F32),
+            pltpu.VMEM((8, 1, COLS), F32),
+            pltpu.VMEM((2, N_X, 16, COLS), BF16),
+            pltpu.VMEM((8, 16, COLS), BF16),
             pltpu.SemaphoreType.DMA((5,)),
             pltpu.SemaphoreType.DMA((3,)),
-            pltpu.SemaphoreType.DMA((11,)),
-            pltpu.SemaphoreType.DMA((11,)),
-            pltpu.SemaphoreType.DMA((N_Z,)),
+            pltpu.SemaphoreType.DMA((13,)),
+            pltpu.SemaphoreType.DMA((13,)),
+            pltpu.SemaphoreType.DMA((5,)),
         ],
         compiler_params=pltpu.CompilerParams(
             collective_id=0, has_side_effects=True, vmem_limit_bytes=60 * 1024 * 1024
@@ -501,7 +595,15 @@
         wv_up.reshape(KVL, VD),
         w_out,
     )
-    return hidden, expert_in.reshape(1, 4, CAP, D)
+    return pl.pallas_call(
+        place_results,
+        out_shape=(
+            jax.ShapeDtypeStruct((1, D), BF16),
+            jax.ShapeDtypeStruct((1, 4, CAP, D), BF16),
+        ),
+        in_specs=[vmem] * 2,
+        out_specs=(vmem, vmem),
+    )(hidden, expert_in)
 
 
 def solution(mesh):

time: 103 us -> 93.8 us (0.911)
  Pallas kernels: 99.3 us -> 93 us
  local copies, waits for them, and re-layouts: 3.1 us -> 0 us
    pallas_call x1, Pallas kernels: 99.3 us -> 91.3 us  [on_device(): pl.pallas_call(kernel, out_shape=(jax.ShapeDtypeStruct((1, D), BF16), jax...]
    reshape x1 -> x0, local copies, waits for them, and re-layouts: 1.72 us -> none  [on_device(): return (hidden, expert_in.reshape(1, 4, CAP, D))]
    pallas_call x0 -> x1, Pallas kernels: none -> 1.71 us  [on_device(): pl.pallas_call(place_results, out_shape=(jax.ShapeDtypeStruct((1, D), BF1...]
    unnamed x1 -> x0, local copies, waits for them, and re-layouts: 1.39 us -> none
where the time goes in v3:
time: 93.8 us; the launch traced here: 93.6 us
  Pallas kernels  93 us (99%)
    pallas_call x1, Pallas kernels, on_device(): pl.pallas_call(kernel, out_shape=(jax.ShapeDtypeStruct((1, D), BF16), jax...  91.3 us

profile of v3, /device:TPU:1, one launch (start us, length us, event | category | flops | bytes accessed | tf_op | source)
XLA Modules:
  0.0 93.6 jit_solution(7651029663516263504)
XLA Ops:
  0.6 91.3 %shard_map.140 = (bf16[1,7168]{1,0:T(2,128)(2,1)}, bf16[16,7168]{1,0:T(8,128)(2,1)}) custom-call(s32[512]{0:T(512)} %owner_s.1, s32[512]{0:T(512)} %lens_s.1, s32[1,512]{1,0:T(1,128)} %bitcast.13, s32[1,512]{1,0:T(1,128)} %bitcast.14, f32[1,32]{1,0:T(1,128)} %constant.8.freqs, s32[8,64]{1,0:T(8,128)} %bitcast.15, bf16[1,7168]{1,0:T(2,128)(2,1)} %residual.1, ...), custom_call_target="tpu_custom_call" | custom-call | flops 600000000 | bytes 8000000 | tf_op jit(solution)/shard_map/pallas_call | solution.py:533
  91.9 1.7 %shard_map.141 = (bf16[1,7168]{1,0:T(2,128)(2,1)}, bf16[1,4,4,7168]{3,2,1,0:T(4,128)(2,1)}) custom-call(bf16[1,7168]{1,0:T(2,128)(2,1)} %get-tuple-element.4.hidden, bf16[16,7168]{1,0:T(8,128)(2,1)} %get-tuple-element.5.expert_in), custom_call_target="tpu_custom_call" | custom-call | tf_op jit(solution)/shard_map/pallas_call | solution.py:598

commit v4 on v3

--- a/solution.py
+++ b/solution.py
@@ -91,7 +91,10 @@
     wq,
     wk,
     wv,
+    stage,
+    ropes,
     kbuf,
+    rbuf,
     qall,
     nlall,
     qsend,
@@ -134,6 +137,7 @@
                 (wk_hbm, wk),
                 (wv_hbm, wv),
                 (nl_hbm, nlall.at[c]),
+                (cache_hbm.at[:, :, pl.ds(KVL, RD)], stage),
             ]
         )
     ]
@@ -165,6 +169,9 @@
     loads[1].wait()
     qall[c] = dot(ql[...], wq[...], 1, 1).astype(BF16)
     loads[4].wait()
+    loads[5].wait()
+    parts = stage[...].astype(F32).reshape(PAIRS, 2, LLOC, RD)
+    ropes[...] = jnp.concatenate([parts[:, 0], parts[:, 1]], 2).astype(BF16)
 
     pl.semaphore_wait(barrier, N_EXP - 1 + (N_CTX - 1) * N_X)
 
@@ -176,10 +183,16 @@
     track("q", qall.at[pl.ds(0, N_CTX - 1)], 0)
 
     pair = lax.rem(e, PAIRS)
-    own = pltpu.make_async_copy(
-        cache_hbm.at[pl.ds(2 * pair, 2)], kbuf.at[NEAR // 2 * N_X + x], recv_sem.at[1]
-    )
-    own.start()
+    def latents(first):
+        return cache_hbm.at[pl.ds(2 * first, 2), :, pl.ds(0, KVL)]
+
+    home = NEAR // 2 * N_X + x
+    own = [
+        pltpu.make_async_copy(latents(pair), kbuf.at[home], recv_sem.at[1]),
+        pltpu.make_async_copy(ropes.at[pair], rbuf.at[home], recv_sem.at[13]),
+    ]
+    for copy in own:
+        copy.start()
 
     def send_cache(i):
         step = i // N_X
@@ -189,12 +202,16 @@
         to_z = lax.rem(z + away, N_Z)
         to_x = lax.rem(x + i + jnp.where(step == NEAR - 1, 1, 0), N_X)
         into = lax.rem(N_Z - away + NEAR // 2, NEAR) * N_X + x
-        pairs = pl.ds(2 * (lax.rem(to_z, NEAR) * N_X + to_x), 2)
-        send(cache_hbm.at[pairs], kbuf.at[into], send_sem.at[1], recv_sem.at[1], (c, to_z * N_X + to_x))
+        first = lax.rem(to_z, NEAR) * N_X + to_x
+        to = (c, to_z * N_X + to_x)
+        send(latents(first), kbuf.at[into], send_sem.at[1], recv_sem.at[1], to)
+        send(ropes.at[first], rbuf.at[into], send_sem.at[13], recv_sem.at[13], to)
 
     each(0, PAIRS - 1, send_cache)
     sent.append((kbuf.at[pl.ds(0, PAIRS - 1)], send_sem.at[1]))
     due["cache"] = (kbuf, recv_sem.at[1])
+    sent.append((rbuf.at[pl.ds(0, PAIRS - 1)], send_sem.at[13]))
+    due["ropes"] = (rbuf, recv_sem.at[13])
 
 
     def send_new(k):
@@ -268,9 +285,9 @@
     earlier = lax.broadcasted_iota(jnp.int32, (ROWS, ROWS), 0) < lax.broadcasted_iota(
         jnp.int32, (ROWS, ROWS), 1
     )
-    stage = lax.broadcasted_iota(jnp.int32, (1, ROWS), 1) // N_X
-    stage = jnp.where(stage == 0, z, z + N_Z - offset(stage, N_Z)) % N_Z
-    held = stage * N_X + lax.broadcasted_iota(jnp.int32, (1, ROWS), 1) % N_X
+    turn = lax.broadcasted_iota(jnp.int32, (1, ROWS), 1) // N_X
+    turn = jnp.where(turn == 0, z, z + N_Z - offset(turn, N_Z)) % N_Z
+    held = turn * N_X + lax.broadcasted_iota(jnp.int32, (1, ROWS), 1) % N_X
     held = one_hot(lax.broadcasted_iota(jnp.int32, (ROWS, ROWS), 0) == held)
     expert = z * 16 + lax.broadcasted_iota(jnp.int32, (16, ROWS), 0)
     line = lax.broadcasted_iota(jnp.int32, (ROWS, 16), 0)
@@ -300,22 +317,30 @@
     pick = (lax.broadcasted_iota(jnp.int32, (16, N_CTX * ROWS), 1) == chosen).astype(F32)
     arrive("new")
     new = dot(pick.astype(BF16), nlall[...].reshape(N_CTX * ROWS, LAT))
+    arrive("cache")
+    arrive("ropes")
+    keys = [kbuf[:, t].astype(F32).reshape(width, KVL).astype(BF16) for t in range(2)]
+    turned_keys = rbuf[...].astype(F32).reshape(width, 2 * RD).astype(BF16)
+    half = lax.broadcasted_iota(jnp.int32, (2 * N_EXP, 2 * RD), 1) < RD
     arrive("own_query")
     arrive("query")
     queries = qrecv[...].reshape(2 * N_EXP, LAT)
     new_scores = dot(queries, new.astype(BF16), 1, 1) * SCALE
     new_scores = jnp.where(even, new_scores[:, 0:1], new_scores[:, 1:2])
     new_scores = jnp.where(e < PAIRS, new_scores, -1e30)
-    arrive("cache")
-    keys = [kbuf[:, t].astype(F32).reshape(width, LAT).astype(BF16) for t in range(2)]
-    scores = jnp.where(even, dot(queries, keys[0], 1, 1), dot(queries, keys[1], 1, 1)) * SCALE
+    latent_part = queries[:, :KVL]
+    turned_part = queries[:, KVL:].astype(F32)
+    turned_part = jnp.concatenate([turned_part, turned_part], 1)
+    turned_part = jnp.where(half == even, turned_part, 0.0).astype(BF16)
+    scores = jnp.where(even, dot(latent_part, keys[0], 1, 1), dot(latent_part, keys[1], 1, 1))
+    scores = (scores + dot(turned_part, turned_keys, 1, 1)) * SCALE
     top = jnp.max(jnp.where(valid, scores, -1e30), 1, keepdims=True)
     top = jnp.maximum(top, new_scores)
     weights = jnp.where(valid, jnp.exp(scores - top), 0.0)
     new_weight = jnp.where(e < PAIRS, jnp.exp(new_scores - top), 0.0)
     total = jnp.sum(weights, 1, keepdims=True) + new_weight
-    mixed = dot(jnp.where(even, weights, 0.0).astype(BF16), keys[0][:, :KVL])
-    mixed = mixed + dot(jnp.where(even, 0.0, weights).astype(BF16), keys[1][:, :KVL])
+    mixed = dot(jnp.where(even, weights, 0.0).astype(BF16), keys[0])
+    mixed = mixed + dot(jnp.where(even, 0.0, weights).astype(BF16), keys[1])
     mixed = mixed + new_weight.astype(BF16).astype(F32) * jnp.where(
         even, new[0:1, :KVL], new[1:2, :KVL]
     )
@@ -543,7 +568,10 @@
             pltpu.VMEM((QW, QL), BF16),
             pltpu.VMEM((NOPE, KVL), BF16),
             pltpu.VMEM((KVL, VD), BF16),
-            pltpu.VMEM((PAIRS, 2, LLOC, LAT), BF16),
+            pltpu.VMEM((N_EXP, LLOC, RD), BF16),
+            pltpu.VMEM((PAIRS, LLOC, 2 * RD), BF16),
+            pltpu.VMEM((PAIRS, 2, LLOC, KVL), BF16),
+            pltpu.VMEM((PAIRS, LLOC, 2 * RD), BF16),
             pltpu.VMEM((N_CTX, ROWS, QW), BF16),
             pltpu.VMEM((N_CTX, ROWS, LAT), BF16),
             pltpu.VMEM((PAIRS, 2, LAT), BF16),
@@ -566,10 +594,10 @@
             pltpu.VMEM((8, 1, COLS), F32),
             pltpu.VMEM((2, N_X, 16, COLS), BF16),
             pltpu.VMEM((8, 16, COLS), BF16),
-            pltpu.SemaphoreType.DMA((5,)),
+            pltpu.SemaphoreType.DMA((6,)),
             pltpu.SemaphoreType.DMA((3,)),
-            pltpu.SemaphoreType.DMA((13,)),
-            pltpu.SemaphoreType.DMA((13,)),
+            pltpu.SemaphoreType.DMA((14,)),
+            pltpu.SemaphoreType.DMA((14,)),
             pltpu.SemaphoreType.DMA((5,)),
         ],
         compiler_params=pltpu.CompilerParams(

time: 93.8 us -> 92.2 us (0.983)
  Pallas kernels: 93 us -> 91.4 us
    pallas_call x1, Pallas kernels: 91.3 us -> 89.7 us  [on_device(): pl.pallas_call(kernel, out_shape=(jax.ShapeDtypeStruct((1, D), BF16), jax...]
where the time goes in v4:
time: 92.2 us; the launch traced here: 92 us
  Pallas kernels  91.4 us (99%)
    pallas_call x1, Pallas kernels, on_device(): pl.pallas_call(kernel, out_shape=(jax.ShapeDtypeStruct((1, D), BF16), jax...  89.7 us

profile of v4, /device:TPU:1, one launch (start us, length us, event | category | flops | bytes accessed | tf_op | source)
XLA Modules:
  0.0 92.0 jit_solution(10353655632776492954)
XLA Ops:
  0.6 89.7 %shard_map.140 = (bf16[1,7168]{1,0:T(2,128)(2,1)}, bf16[16,7168]{1,0:T(8,128)(2,1)}) custom-call(s32[512]{0:T(512)} %owner_s.1, s32[512]{0:T(512)} %lens_s.1, s32[1,512]{1,0:T(1,128)} %bitcast.13, s32[1,512]{1,0:T(1,128)} %bitcast.14, f32[1,32]{1,0:T(1,128)} %constant.8.freqs, s32[8,64]{1,0:T(8,128)} %bitcast.15, bf16[1,7168]{1,0:T(2,128)(2,1)} %residual.1, ...), custom_call_target="tpu_custom_call" | custom-call | flops 600000000 | bytes 8000000 | tf_op jit(solution)/shard_map/pallas_call | solution.py:558
  90.3 1.7 %shard_map.141 = (bf16[1,7168]{1,0:T(2,128)(2,1)}, bf16[1,4,4,7168]{3,2,1,0:T(4,128)(2,1)}) custom-call(bf16[1,7168]{1,0:T(2,128)(2,1)} %get-tuple-element.4.hidden, bf16[16,7168]{1,0:T(8,128)(2,1)} %get-tuple-element.5.expert_in), custom_call_target="tpu_custom_call" | custom-call | tf_op jit(solution)/shard_map/pallas_call | solution.py:626

commit v5 on v4

--- a/solution.py
+++ b/solution.py
@@ -70,7 +70,6 @@
 
 
 def kernel(
-    owner_s,
     lens_s,
     owner_row,
     lens_row,
@@ -95,8 +94,11 @@
     ropes,
     kbuf,
     rbuf,
-    qall,
-    nlall,
+    nl,
+    qout,
+    qgot,
+    nlout,
+    nlgot,
     qsend,
     qrecv,
     lsend,
@@ -136,7 +138,7 @@
                 (wq_hbm, wq),
                 (wk_hbm, wk),
                 (wv_hbm, wv),
-                (nl_hbm, nlall.at[c]),
+                (nl_hbm, nl),
                 (cache_hbm.at[:, :, pl.ds(KVL, RD)], stage),
             ]
         )
@@ -144,6 +146,30 @@
     for load in loads:
         load.start()
 
+    square_row = lax.broadcasted_iota(jnp.int32, (ROWS, ROWS), 0)
+    square_column = lax.broadcasted_iota(jnp.int32, (ROWS, ROWS), 1)
+    eye, earlier = square_row == square_column, square_row < square_column
+    slot_line = lax.broadcasted_iota(jnp.int32, (N_CTX * SLOTS, ROWS), 0)
+
+    def upright(row):
+        return jnp.sum(jnp.where(eye, row, 0.0), 1, keepdims=True)
+
+    def count(mask):
+        return jnp.sum(jnp.where(mask, 1.0, 0.0), 0, keepdims=True)
+
+    def slots_of(part, rank):
+        return one_hot(slot_line == (part * SLOTS + rank).astype(jnp.int32))
+
+    request = lax.broadcasted_iota(jnp.int32, (ROWS, N_CTX * ROWS), 1)
+    held = owner_row[...] == c * ROWS + lax.broadcasted_iota(jnp.int32, request.shape, 0)
+    shard = jnp.sum(jnp.where(held, (request // ROWS).astype(F32), 0.0), 1, keepdims=True)
+    shard_row = jnp.sum(jnp.where(eye, shard, 0.0), 0, keepdims=True)
+    outbound = slots_of(shard_row, count((shard == shard_row) & earlier))
+    mine = own_part(owner_row[...], y, core)
+    owner, target = (mine // ROWS).astype(F32), mine.astype(F32)
+    lower = (upright(owner) == owner) & (upright(target) < target)
+    inbound = slots_of(owner, count(lower))
+
     barrier = pltpu.get_barrier_semaphore()
     sent, due = [], {}
 
@@ -167,7 +193,9 @@
 
     loads[0].wait()
     loads[1].wait()
-    qall[c] = dot(ql[...], wq[...], 1, 1).astype(BF16)
+    q = dot(ql[...], wq[...], 1, 1).astype(BF16)
+    qout[...] = dot(outbound, q).astype(BF16).reshape(N_CTX, SLOTS, QW)
+    qgot[c] = qout[c]
     loads[4].wait()
     loads[5].wait()
     parts = stage[...].astype(F32).reshape(PAIRS, 2, LLOC, RD)
@@ -176,11 +204,11 @@
     pl.semaphore_wait(barrier, N_EXP - 1 + (N_CTX - 1) * N_X)
 
     def send_q(k):
-        to = (lax.rem(c + offset(k, N_CTX), N_CTX), e)
-        send(qall.at[c], qall.at[c], send_sem.at[0], recv_sem.at[0], to)
+        to = lax.rem(c + offset(k, N_CTX), N_CTX)
+        send(qout.at[to], qgot.at[c], send_sem.at[0], recv_sem.at[0], (to, e))
 
     each(1, N_CTX, send_q)
-    track("q", qall.at[pl.ds(0, N_CTX - 1)], 0)
+    track("q", qgot.at[pl.ds(0, N_CTX - 1)], 0)
 
     pair = lax.rem(e, PAIRS)
     def latents(first):
@@ -214,12 +242,15 @@
     due["ropes"] = (rbuf, recv_sem.at[13])
 
 
+    nlout[...] = dot(outbound, nl[...]).astype(BF16).reshape(N_CTX, SLOTS, LAT)
+    nlgot[c] = nlout[c]
+
     def send_new(k):
-        to = (lax.rem(c + offset(k, N_CTX), N_CTX), e)
-        send(nlall.at[c], nlall.at[c], send_sem.at[2], recv_sem.at[2], to)
+        to = lax.rem(c + offset(k, N_CTX), N_CTX)
+        send(nlout.at[to], nlgot.at[c], send_sem.at[2], recv_sem.at[2], (to, e))
 
     each(1, N_CTX, send_new)
-    track("new", nlall.at[pl.ds(0, N_CTX - 1)], 2)
+    track("new", nlgot.at[pl.ds(0, N_CTX - 1)], 2)
 
     mine_row, block = core * N_X + x, x * 2 + core
     for i in range(8):
@@ -237,17 +268,12 @@
     send(ids, other_ids, send_sem.at[11], recv_sem.at[11], (y * 2 + 1 - core, e))
     track("ids", other_ids, 11)
 
-    mine = own_part(owner_row[...], y, core)
-    place = (lax.broadcasted_iota(jnp.int32, (N_CTX * ROWS, ROWS), 0) == mine).astype(F32)
     lengths = own_part(lens_row[...], y, core).astype(F32)
-    eye = lax.broadcasted_iota(jnp.int32, (ROWS, ROWS), 0) == lax.broadcasted_iota(
-        jnp.int32, (ROWS, ROWS), 1
-    )
-    angles = jnp.sum(jnp.where(eye, lengths, 0.0), 1, keepdims=True) * freqs[...]
+    angles = upright(lengths) * freqs[...]
     cosines, sines = jnp.cos(angles), jnp.sin(angles)
     loads[2].wait()
     arrive("q")
-    q = dot(place.astype(BF16), qall[...].reshape(N_CTX * ROWS, QW), 0, 0)
+    q = dot(inbound, qgot[...].reshape(N_CTX * SLOTS, QW), 0, 0)
     absorbed = dot(q[:, :NOPE].astype(BF16), wk[...])
     first, second = q[:, NOPE : NOPE + RD // 2], q[:, NOPE + RD // 2 :]
     turned = jnp.concatenate(
@@ -282,9 +308,6 @@
     track("w", wbuf.at[pl.ds(0, N_X - 1)], 3)
 
     arrive("ids")
-    earlier = lax.broadcasted_iota(jnp.int32, (ROWS, ROWS), 0) < lax.broadcasted_iota(
-        jnp.int32, (ROWS, ROWS), 1
-    )
     turn = lax.broadcasted_iota(jnp.int32, (1, ROWS), 1) // N_X
     turn = jnp.where(turn == 0, z, z + N_Z - offset(turn, N_Z)) % N_Z
     held = turn * N_X + lax.broadcasted_iota(jnp.int32, (1, ROWS), 1) % N_X
@@ -312,11 +335,11 @@
     position = position + lax.broadcasted_iota(jnp.int32, (1, width), 1) % LLOC
     even = lax.broadcasted_iota(jnp.int32, (2 * N_EXP, 1), 0) % 2 == 0
     valid = position < jnp.where(even, lens_s[first_request], lens_s[first_request + 1])
-    chosen = lax.broadcasted_iota(jnp.int32, (16, 1), 0)
-    chosen = jnp.where(chosen == 0, owner_s[first_request], owner_s[first_request + 1])
-    pick = (lax.broadcasted_iota(jnp.int32, (16, N_CTX * ROWS), 1) == chosen).astype(F32)
+    wanted = 2 * pair + jnp.minimum(lax.broadcasted_iota(jnp.int32, (16, ROWS), 0), 1)
+    pick = one_hot(lax.broadcasted_iota(jnp.int32, (16, ROWS), 1) == wanted)
+    pick = dot(pick, inbound, 1, 1).astype(BF16)
     arrive("new")
-    new = dot(pick.astype(BF16), nlall[...].reshape(N_CTX * ROWS, LAT))
+    new = dot(pick, nlgot[...].reshape(N_CTX * SLOTS, LAT))
     arrive("cache")
     arrive("ropes")
     keys = [kbuf[:, t].astype(F32).reshape(width, KVL).astype(BF16) for t in range(2)]
@@ -365,12 +388,9 @@
     track("latent", lrecv.at[pl.ds(0, N_EXP - 1)], 5)
 
     def ranks(owner):
-        rows = jnp.sum(jnp.where(eye, owner, 0.0), 1, keepdims=True)
-        return jnp.sum(jnp.where((rows == owner) & earlier, 1.0, 0.0), 0, keepdims=True)
-
-    owner = (mine // ROWS).astype(F32)
-    key = (owner * SLOTS + ranks(owner)).astype(jnp.int32)
-    bucket = one_hot(lax.broadcasted_iota(jnp.int32, (N_CTX * SLOTS, ROWS), 0) == key)
+        return count((upright(owner) == owner) & earlier)
+
+    bucket = slots_of(owner, ranks(owner))
     keys = []
     for i in range(N_CTX):
         owner = owner_row[:, i * ROWS : (i + 1) * ROWS] // ROWS
@@ -504,13 +524,12 @@
     for g in range(2):
         rows = dot(selection[g], zbuf[:, g].reshape(ROWS, COLS)).astype(BF16)
         slots[g] = rows.reshape(N_X, 16, COLS)
-
-    def send_slots(k):
-        to_x, to_core = lax.rem(x + k // 2, N_X), lax.rem(core + k, 2)
-        to = (y * 2 + to_core, z * N_X + to_x)
-        send(slots.at[to_core, to_x], gbuf.at[block], send_sem.at[10], recv_sem.at[10], to)
-
-    each(1, 8, send_slots)
+        for i in range(1, N_X):
+            to_x = lax.rem(x + i, N_X)
+            to = (y * 2 + g, z * N_X + to_x)
+            send(slots.at[g, to_x], gbuf.at[block], send_sem.at[10], recv_sem.at[10], to)
+    to = (y * 2 + 1 - core, e)
+    send(slots.at[1 - core, x], gbuf.at[block], send_sem.at[10], recv_sem.at[10], to)
     track("slots", gbuf.at[pl.ds(0, 7)], 10)
     gbuf[block] = slots[core, x]
     arrive("row")
@@ -561,7 +580,7 @@
             jax.ShapeDtypeStruct((1, D), BF16),
             jax.ShapeDtypeStruct((4 * CAP, D), BF16),
         ),
-        in_specs=[smem] * 2 + [vmem] * 6 + [anywhere] * 7,
+        in_specs=[smem] + [vmem] * 6 + [anywhere] * 7,
         out_specs=(vmem, vmem),
         scratch_shapes=[
             pltpu.VMEM((ROWS, QL), BF16),
@@ -572,8 +591,11 @@
             pltpu.VMEM((PAIRS, LLOC, 2 * RD), BF16),
             pltpu.VMEM((PAIRS, 2, LLOC, KVL), BF16),
             pltpu.VMEM((PAIRS, LLOC, 2 * RD), BF16),
-            pltpu.VMEM((N_CTX, ROWS, QW), BF16),
-            pltpu.VMEM((N_CTX, ROWS, LAT), BF16),
+            pltpu.VMEM((ROWS, LAT), BF16),
+            pltpu.VMEM((N_CTX, SLOTS, QW), BF16),
+            pltpu.VMEM((N_CTX, SLOTS, QW), BF16),
+            pltpu.VMEM((N_CTX, SLOTS, LAT), BF16),
+            pltpu.VMEM((N_CTX, SLOTS, LAT), BF16),
             pltpu.VMEM((PAIRS, 2, LAT), BF16),
             pltpu.VMEM((N_EXP, 2, LAT), BF16),
             pltpu.VMEM((N_EXP, 2, KVL + 128), BF16),
@@ -607,7 +629,6 @@
             flops=600_000_000, bytes_accessed=8_000_000, transcendentals=40_000
         ),
     )(
-        owner_slot,
         cached_len,
         owner_slot.reshape(1, N_CTX * ROWS),
         cached_len.reshape(1, N_CTX * ROWS),

time: 92.2 us -> 91.8 us (level)
  no operation moved by 1% of the time
where the time goes in v5:
time: 91.8 us; the launch traced here: 91.6 us
  Pallas kernels  91 us (99%)
    pallas_call x1, Pallas kernels, on_device(): pl.pallas_call(kernel, out_shape=(jax.ShapeDtypeStruct((1, D), BF16), jax...  89.3 us

profile of v5, /device:TPU:1, one launch (start us, length us, event | category | flops | bytes accessed | tf_op | source)
XLA Modules:
  0.0 91.6 jit_solution(1961715459979608581)
XLA Ops:
  0.6 89.3 %shard_map.140 = (bf16[1,7168]{1,0:T(2,128)(2,1)}, bf16[16,7168]{1,0:T(8,128)(2,1)}) custom-call(s32[512]{0:T(512)} %lens_s.1, s32[1,512]{1,0:T(1,128)} %bitcast.15, s32[1,512]{1,0:T(1,128)} %bitcast.13, f32[1,32]{1,0:T(1,128)} %constant.8.freqs, s32[8,64]{1,0:T(8,128)} %bitcast.14, bf16[1,7168]{1,0:T(2,128)(2,1)} %residual.1, f32[1,7168]{1,0:T(1,128)} %bitcast.12, ...), custom_call_target="tpu_custom_call" | custom-call | flops 600000000 | bytes 8000000 | tf_op jit(solution)/shard_map/pallas_call | solution.py:577
  89.9 1.7 %shard_map.141 = (bf16[1,7168]{1,0:T(2,128)(2,1)}, bf16[1,4,4,7168]{3,2,1,0:T(4,128)(2,1)}) custom-call(bf16[1,7168]{1,0:T(2,128)(2,1)} %get-tuple-element.4.hidden, bf16[16,7168]{1,0:T(8,128)(2,1)} %get-tuple-element.5.expert_in), custom_call_target="tpu_custom_call" | custom-call | tf_op jit(solution)/shard_map/pallas_call | solution.py:647

commit v6 on v5

--- a/solution.py
+++ b/solution.py
@@ -493,8 +493,8 @@
     pass_on(0, 8, 4, z_sem.at[3])
     pass_on(0, 9, -4, z_sem.at[4])
     for j in range(1, 4):
-        pass_on(0, 16 - 2 * j, j, recv_sem.at[9])
-        pass_on(0, 17 - 2 * j, -j, recv_sem.at[9])
+        pass_on(0, 16 - 2 * j, j, z_sem.at[5])
+        pass_on(0, 17 - 2 * j, -j, z_sem.at[5])
 
     osend[:, 0, :] = hidden
     orecv[block] = osend[mine_row]
@@ -518,11 +518,17 @@
         for j in range(3):
             pass_on(8 + side, 2 + 2 * j + side, (3 - j) * way, recv_sem.at[9])
     sent.append((zbuf.at[pl.ds(0, N_Z - 1)], send_sem.at[9]))
-    due["columns"] = (zbuf.at[pl.ds(0, N_Z - 3)], recv_sem.at[9])
+    due["columns"] = (zbuf.at[pl.ds(0, 7)], recv_sem.at[9])
+    drain(zbuf.at[pl.ds(10, 6)], z_sem.at[5])
+    part = ROWS // 2
+    near_rows = [
+        dot(selection[g, :, part:], zbuf[8:, g].reshape(part, COLS)) for g in range(2)
+    ]
 
     arrive("columns")
     for g in range(2):
-        rows = dot(selection[g], zbuf[:, g].reshape(ROWS, COLS)).astype(BF16)
+        rows = dot(selection[g, :, :part], zbuf[:8, g].reshape(part, COLS))
+        rows = (rows + near_rows[g]).astype(BF16)
         slots[g] = rows.reshape(N_X, 16, COLS)
         for i in range(1, N_X):
             to_x = lax.rem(x + i, N_X)
@@ -620,7 +626,7 @@
             pltpu.SemaphoreType.DMA((3,)),
             pltpu.SemaphoreType.DMA((14,)),
             pltpu.SemaphoreType.DMA((14,)),
-            pltpu.SemaphoreType.DMA((5,)),
+            pltpu.SemaphoreType.DMA((6,)),
         ],
         compiler_params=pltpu.CompilerParams(
             collective_id=0, has_side_effects=True, vmem_limit_bytes=60 * 1024 * 1024

time: 91.8 us -> 92 us (level)
  no operation moved by 1% of the time
where the time goes in v6:
time: 92 us; the launch traced here: 91.8 us
  Pallas kernels  91.2 us (99%)
    pallas_call x1, Pallas kernels, on_device(): pl.pallas_call(kernel, out_shape=(jax.ShapeDtypeStruct((1, D), BF16), jax...  89.4 us

profile of v6, /device:TPU:1, one launch (start us, length us, event | category | flops | bytes accessed | tf_op | source)
XLA Modules:
  0.0 91.8 jit_solution(17803140805516860138)
XLA Ops:
  0.6 89.4 %shard_map.140 = (bf16[1,7168]{1,0:T(2,128)(2,1)}, bf16[16,7168]{1,0:T(8,128)(2,1)}) custom-call(s32[512]{0:T(512)} %lens_s.1, s32[1,512]{1,0:T(1,128)} %bitcast.15, s32[1,512]{1,0:T(1,128)} %bitcast.13, f32[1,32]{1,0:T(1,128)} %constant.8.freqs, s32[8,64]{1,0:T(8,128)} %bitcast.14, bf16[1,7168]{1,0:T(2,128)(2,1)} %residual.1, f32[1,7168]{1,0:T(1,128)} %bitcast.12, ...), custom_call_target="tpu_custom_call" | custom-call | flops 600000000 | bytes 8000000 | tf_op jit(solution)/shard_map/pallas_call | solution.py:583
  90.1 1.7 %shard_map.141 = (bf16[1,7168]{1,0:T(2,128)(2,1)}, bf16[1,4,4,7168]{3,2,1,0:T(4,128)(2,1)}) custom-call(bf16[1,7168]{1,0:T(2,128)(2,1)} %get-tuple-element.4.hidden, bf16[16,7168]{1,0:T(8,128)(2,1)} %get-tuple-element.5.expert_in), custom_call_target="tpu_custom_call" | custom-call | tf_op jit(solution)/shard_map/pallas_call | solution.py:653
